TPU v7x, 512 devices: a whole 4x4x16 slice. The times are simulated.
512 devices in a mesh: req: 32 (over x, y, core), tp: 16 (over z).
Axes of the slice: x: 4, y: 4, z: 16, core: 2. Of those that a mesh axis runs over, the one named last changes fastest.
Arguments:
- queries: bfloat16 [64, 8192], P('req'), may hold values from -8 to 8
- image_cache: bfloat16 [32, 1664, 2048], P('req', 'tp'), may hold values from -12 to 12
- image_lists: int32 [64, 4], replicated, may hold values from 0 to 31, as said below
- cited_count: int32 [64], replicated, may hold values from 1 to 4, as said below
- image_slot: int32 [32], replicated, may hold values from 0 to 31, as said below
Outputs:
- attended: float32 [64, 8192], P('req', 'tp')
Inputs may be any that keep to these rules, and one draw needn't show every extreme that they name: `image_lists`: the 4 image ids of a row are different; entry 0 of request r names an image whose storage slot is held by the index of req before that of request r (counted round). `cited_count`: some request cites 4 images and some request one. `image_slot`: every slot holds exactly one image.
All inputs are finite; a program needn't handle non-finite values.
Results may differ from a plain program's by a relative error of at most 0.0007.
Values may be sent and summed in bfloat16 or wider, within the bound.
A program may use at most 128 MiB of HBM per device.

v0:
```python
import math

import jax
import jax.numpy as jnp
from jax import lax
from jax.sharding import PartitionSpec as P

HEADS = 64
KVH = 8
HD = 128
IMG_TOK = 1601


negative_floor = -1e30


def citations(lists, counts, slot_table):
    images_total = slot_table.shape[0]
    onehot = lists[:, :, None] == jnp.arange(images_total, dtype=jnp.int32)[None, None, :]
    slots = jnp.sum(jnp.where(onehot, slot_table[None, None, :], 0), axis=2)
    listed = jnp.arange(lists.shape[1], dtype=jnp.int32)[None, :] < counts[:, None]
    return (slots, listed)


def citing(slots, listed, slot_ids):
    matches = (slots[:, :, None] == slot_ids[None, None, :]) & listed[:, :, None]
    return jnp.any(matches, axis=1)


def split_cache(portion):
    amount = portion.shape[0]
    token_block = portion.shape[1]
    keys = portion[:, :, : KVH * HD].reshape(amount, token_block, KVH, HD)
    values = portion[:, :, KVH * HD :].reshape(amount, token_block, KVH, HD)
    return (keys, values)


def block_scores(grouped, keys):
    raw = jnp.einsum("rkgd,ntkd->rkgnt", grouped, keys, preferred_element_type=jnp.float32)
    return raw * (1.0 / math.sqrt(HD))


def weigh_values(weights, values):
    return jnp.einsum(
        "rkgnt,ntkd->rkgd", weights, values.astype(jnp.float32), precision=lax.Precision.HIGHEST
    )


def absorb_slots(running, portion, slot_ids, grouped, own_slots, own_listed, token_ok):
    maxima, totals, weighted = running
    keys, values = split_cache(portion)
    scores = block_scores(grouped, keys)
    allowed = (
        citing(own_slots, own_listed, slot_ids)[:, None, None, :, None]
        & token_ok[None, None, None, None, :]
    )
    scores = jnp.where(allowed, scores, negative_floor)
    updated = jnp.maximum(maxima, jnp.max(scores, axis=(3, 4)))
    weights = jnp.where(allowed, jnp.exp(scores - updated[:, :, :, None, None]), 0.0)
    totals = jnp.sum(weights, axis=(3, 4))
    weighted = weigh_values(weights, values)
    return (updated, totals, weighted)


def finish_heads(maxima, totals, weighted, rows):
    highest = lax.pmax(maxima, "tp")
    factor = jnp.exp(maxima - highest)
    totals = (totals * factor).reshape(rows, HEADS)
    weighted = (weighted * factor[:, :, :, None]).reshape(rows, HEADS * HD)
    return (
        lax.psum_scatter(weighted, "tp", scatter_dimension=1, tiled=True),
        lax.psum_scatter(totals, "tp", scatter_dimension=1, tiled=True),
    )


def per_device(queries, image_cache, image_lists, cited_count, image_slot):
    rows = queries.shape[0]
    heads_here = HEADS // lax.axis_size("tp")
    token_block = image_cache.shape[1]
    token_ids = lax.axis_index("tp") * token_block + jnp.arange(token_block, dtype=jnp.int32)
    token_ok = token_ids < IMG_TOK
    slots, listed = citations(image_lists, cited_count, image_slot)
    first_row = lax.axis_index("req") * rows
    own_slots = lax.dynamic_slice_in_dim(slots, first_row, rows, 0)
    own_listed = lax.dynamic_slice_in_dim(listed, first_row, rows, 0)
    grouped = queries.reshape(rows, KVH, HEADS // KVH, HD)
    start_max = jnp.full((rows, KVH, HEADS // KVH), negative_floor, jnp.float32)
    start_sum = jnp.zeros((rows, KVH, HEADS // KVH), jnp.float32)
    start_values = jnp.zeros((rows, KVH, HEADS // KVH, HD), jnp.float32)
    running = (start_max, start_sum, start_values)
    portion = lax.all_gather(image_cache, "req", axis=0, tiled=True)
    slot_ids = jnp.arange(portion.shape[0], dtype=jnp.int32)
    running = absorb_slots(running, portion, slot_ids, grouped, own_slots, own_listed, token_ok)
    maxima, totals, weighted = running
    weighted, totals = finish_heads(maxima, totals, weighted, rows)
    attended = weighted.reshape(rows, heads_here, HD) / totals[:, :, None]
    return attended.reshape(rows, heads_here * HD)


def solution(mesh):
    return jax.shard_map(
        per_device,
        mesh=mesh,
        in_specs=(P("req", None), P("req", "tp", None), P(), P(), P()),
        out_specs=P("req", "tp"),
        check_vma=False,
    )
```

profile of v0, /device:TPU:14, one launch (start us, length us, event | category | flops | bytes accessed | tf_op | source)
XLA Modules:
  0.0 246.8 jit_solution(3834731303353509693)
XLA Ops:
  6.5 0.7 all-gather.2.cloned.1.call-update
  7.3 0.0 reduce-scatter.5.cloned.1.call-start
  7.3 0.8 select_reduce_fusion
  8.1 0.1 constant_dynamic-slice_fusion.1
  8.2 0.1 copy.26
  8.3 0.7 dynamic-slice.2
  9.0 0.1 iota_compare_fusion.2
  9.1 0.1 fusion.20
  9.2 0.1 copy.27
  9.3 1.3 dynamic-slice
  11.2 0.1 broadcast_and_fusion
  11.3 82.6 %all-gather.2.cloned.1.call-done = bf16[32,104,2048]{2,1,0:T(8,128)(2,1)} async-done(((bf16[1,104,2048]{2,1,0:T(8,128)(2,1)}), bf16[32,104,2048]{2,1,0:T(8,128)(2,1)}) %all-gather.2.cloned.1.call-update) | async-done | bytes 13631504 | tf_op jit(solution)/shard_map/all_gather | solution.py:91
  93.9 8.2 %fusion.25 = (bf16[32,104,1024]{2,1,0:T(8,128)(2,1)S(1)}, bf16[32,104,1024]{2,1,0:T(8,128)(2,1)}) fusion(bf16[32,104,2048]{2,1,0:T(8,128)(2,1)} %all-gather.2.cloned.1.call-done), kind=kLoop, calls=%fused_computation.38 | loop fusion | bytes 27262976 | tf_op jit(solution)/shard_map/slice | solution.py:33
  102.1 4.7 %copy.51 = bf16[416,8,8,128]{3,2,1,0:T(8,128)(2,1)S(1)} copy(bf16[416,8,8,128]{3,1,2,0:T(8,128)(2,1)} %bitcast.69) | data formatting | bytes 13631488
  106.8 3.3 %bitcast_bitcast_fusion = bf16[32,104,8,128,1]{3,2,1,0,4:T(8,128)(2,1)} fusion(bf16[32,104,8,128]{3,2,1,0:T(8,128)(2,1)S(1)} %bitcast.66), kind=kLoop, calls=%fused_computation | loop fusion | bytes 13631488 | tf_op jit(solution)/shard_map/reshape | solution.py:34
  110.1 1.8 copy.49
  111.8 0.0 copy-start
  111.8 0.5 bitcast_bitcast_fusion.1
  112.3 0.3 copy-done
  112.6 4.1 %fusion.5 = (f32[2,8,8]{2,0,1:T(2,128)S(1)}, f32[8,32,104,2,8]{2,4,3,1,0:T(8,128)S(1)}) fusion(pred[2,32,104]{2,0,1:T(4,128)(4,1)S(1)} %broadcast_and_fusion, bf16[32,104,8,128,1]{3,2,1,0,4:T(8,128)(2,1)S(1)} %bitcast_bitcast_fusion.1, bf16[1,2,64,128]{3,1,2,0:T(2,128)(2,1)S(1)} %bitcast.72), kind=kOutput, calls=%fused_computation.9 | convolution fusion | flops 110329728 | bytes 8559616 | tf_op jit(solution)/shard_map/rkgd,ntkd->rkgnt/dot_general | solution.py:39
  116.7 32.0 %pmax.7 = f32[2,8,8]{2,0,1:T(2,128)S(1)} all-reduce(f32[2,8,8]{2,0,1:T(2,128)S(1)} %broadcast_maximum_fusion), channel_id=1, replica_groups=mesh['req'=32,'tp'=16] {'tp'}, use_global_device_ids=true, to_apply=%region_3.4 | all-reduce | flops 128 | bytes 1024 | tf_op jit(solution)/shard_map/pmax | solution.py:66
  148.7 0.9 fusion.6
  149.6 8.2 %fusion.10 = f32[2,8,8,128]{3,2,0,1:T(8,128)S(1)} fusion(bf16[32,104,8,128,1]{3,2,1,0,4:T(8,128)(2,1)} %bitcast_bitcast_fusion, f32[8,32,104,2,8]{2,4,3,1,0:T(8,128)S(1)} %get-tuple-element.10, f32[2,8,8]{2,0,1:T(2,128)S(1)} %broadcast_maximum_fusion, pred[2,32,104]{2,0,1:T(4,128)(4,1)S(1)} %broadcast_and_fusion, f32[2,8,8]{2,0,1:T(2,128)S(1)} %get-tuple-element.6), kind=kOutput, calls=%fused_computation.12 | convolution fusion | flops 656031744 | bytes 8592896 | tf_op jit(solution)/shard_map/rkgnt,ntkd->rkgd/dot_general | solution.py:44
  157.8 2.6 %copy.47 = f32[2,8,8,128]{0,3,2,1:T(8,128)} copy(f32[2,8,8,128]{3,2,0,1:T(8,128)S(1)} %fusion.10) | data formatting | bytes 131072
  160.4 0.0 reduce-scatter.5.cloned.1.call-update
  160.4 0.1 reshape.44
  160.5 28.5 %all-reduce = f32[2,64]{1,0:T(2,128)S(1)} all-reduce(f32[2,64]{1,0:T(2,128)S(1)} %reshape.44), channel_id=3, replica_groups=mesh['req'=32,'tp'=16] {'tp'}, use_global_device_ids=true, to_apply=%region_6.7.clone | all-reduce | flops 128 | bytes 1024
  189.0 0.1 constant_dynamic-slice_fusion
  189.1 0.1 broadcast_bitcast_fusion
  189.1 49.1 %reduce-scatter.5.cloned.1.call-done = f32[512,2]{1,0:T(8,128)} async-done(((f32[8192,2]{1,0:T(8,128)}), f32[512,2]{1,0:T(8,128)}) %reduce-scatter.5.cloned.1.call-update) | async-done | bytes 4112
  238.2 1.1 copy.45
  239.3 0.6 bitcast_divide_fusion
  (5 shorter events, 0.0 us)
Async XLA Ops:
  6.5 87.4 %all-gather.2.cloned.1.call-start = ((), (), s32[]{:S(2)}) async-start(), calls=%async_computation.1 | async-start | bytes 14057472 | tf_op jit(solution)/shard_map/all_gather | solution.py:91
  7.3 231.0 %reduce-scatter.5.cloned.1.call-start = ((), (), s32[]{:S(2)}) async-start(), calls=%async_computation.2 | async-start | bytes 4456448
  111.8 0.8 copy-start
Sparse Core Ops, SparseCore 0:
  10.5 83.4 all-gather.1
  160.5 77.6 reduce-scatter.4
where the time goes:
time: 247 us
  waiting for transfers between devices  132 us (53%)
  blocking collectives  60.4 us (24%)
  local copies, waits for them, and re-layouts  24.8 us (10%)
  between operations  14.1 us (6%)
  matrix products  12.3 us (5%)
  other arithmetic  2.57 us (1%)
    all_gather x1, waiting for transfers between devices, per_device(): portion = lax.all_gather(image_cache, 'req', axis=0, tiled=True)  82.6 us
    unnamed x3, waiting for transfers between devices  49.8 us
    pmax x1, blocking collectives, finish_heads(): highest = lax.pmax(maxima, 'tp')  32 us
    unnamed x1, blocking collectives  28.5 us
    unnamed x9, local copies, waits for them, and re-layouts  11.8 us
    dot_general x1, matrix products, weigh_values(): jnp.einsum('rkgnt,ntkd->rkgd', weights, values.astype(jnp.float32), preci...  8.19 us
    slice x1, local copies, waits for them, and re-layouts, split_cache(): keys = portion[:, :, :KVH * HD].reshape(amount, token_block, KVH, HD)  8.15 us
  transfers between devices with their start and end apart: 2, of which 2 were waited for; matrix products, arithmetic and copies ran while one was open for 1% of the time, Pallas kernels for 0%

commit v1 on v0

v1 whole, which is shorter than its diff:
```python
import functools
import math

import jax
import jax.numpy as jnp
from jax import lax
from jax.experimental import pallas as pl
from jax.experimental.pallas import tpu as pltpu
from jax.sharding import PartitionSpec as P

KVH = 8
GROUP = 8
HD = 128
IMG_TOK = 1601
LISTS = 4
NX = 4
NY = 4
NZ = 16
CHIPS = NX * NY
TOK = 104
TOK_SENT = 112
SEG = 128
SEGS = 4
KV_HERE = KVH // 2
ROWS = 16
BLOCK = KV_HERE * ROWS
NEG = -1e30
SCALE = math.log2(math.e) / math.sqrt(HD)
MESH = pl.DeviceIdType.MESH
OFFSETS = sorted(
    ((i, j) for i in range(NX) for j in range(NY) if (i, j) != (0, 0)),
    key=lambda o: -(min(o[0], NX - o[0]) + min(o[1], NY - o[1])),
)
NEAR = tuple(d for d in range(-4, 5) if d)


def wait_bytes(ref, sem):
    pltpu.make_async_copy(ref, ref, sem).wait()


def kernel(
    q_ref, cache_ref, lists_ref, count_ref, slot_ref, out_ref,
    qbuf, kbuf, vbuf, ksend, vsend, bias, obuf, rbuf, zsend, zbuf,
    g_send, g_recv, kv_send, kv_recv, r_send, r_recv, z_send, z_recv, z_ready,
):
    req = lax.axis_index("req")
    z = lax.axis_index("tp")
    chip = lax.div(req, 2)
    core = lax.rem(req, 2)
    x = lax.div(chip, NY)
    y = lax.rem(chip, NY)
    par = lax.rem(z, 2)

    def device(x_, y_, c_, z_):
        return ((x_ * NY + y_) * 2 + c_, z_)

    def moved(dx, dy):
        return lax.rem(x + dx, NX), lax.rem(y + dy, NY)

    other_core = device(x, y, 1 - core, z)
    other_slice = device(x, y, core, z + 1 - 2 * par)

    barrier = pltpu.get_barrier_semaphore()
    met = [other_core]
    met += [device(*moved(dx, dy), core, z) for dx, dy in OFFSETS]
    met += [device(x, y, core, lax.rem(z + d + NZ, NZ)) for d in NEAR]
    for there in met:
        pl.semaphore_signal(barrier, inc=1, device_id=there, device_id_type=MESH)

    half = KV_HERE * GROUP * HD
    own = q_ref[:, pl.ds(pl.multiple_of(par * half, half), half)].astype(jnp.float32)
    for k in range(KV_HERE):
        rows = [
            own[r : r + 1, (k * GROUP + g) * HD : (k * GROUP + g + 1) * HD]
            for r in range(2)
            for g in range(GROUP)
        ]
        qbuf[chip, k * ROWS : (k + 1) * ROWS, :] = jnp.concatenate(rows, axis=0).astype(jnp.bfloat16)

    zeros = jnp.zeros((32, HD), jnp.bfloat16)
    for s in range(SEGS):
        for k in range(KV_HERE):
            kbuf[s, k, TOK_SENT:, :] = zeros[: SEG - TOK_SENT]
            vbuf[s, k, TOK_SENT:, :] = zeros[: SEG - TOK_SENT]
    tail = jnp.zeros((TOK_SENT - TOK, HD), jnp.bfloat16)
    for k in range(KV_HERE):
        for buf, base in ((kbuf, 0), (vbuf, KVH * HD)):
            at = pl.multiple_of(base + (par * KV_HERE + k) * HD, HD)
            part = cache_ref[0, :, pl.ds(at, HD)]
            buf[0, k, :TOK_SENT, :] = jnp.concatenate([part, tail], axis=0)
        for buf, base in ((ksend, 0), (vsend, KVH * HD)):
            at = pl.multiple_of(base + ((1 - par) * KV_HERE + k) * HD, HD)
            part = cache_ref[0, :, pl.ds(at, HD)]
            buf[k] = jnp.concatenate([part, tail], axis=0)

    pl.semaphore_wait(barrier, len(met))
    for d in (-4, 4):
        there = device(x, y, core, lax.rem(z + d + NZ, NZ))
        pl.semaphore_signal(z_ready, inc=1, device_id=there, device_id_type=MESH)

    def remote(src, dst, send, recv, there):
        return pltpu.make_async_remote_copy(
            src_ref=src, dst_ref=dst, send_sem=send, recv_sem=recv,
            device_id=there, device_id_type=MESH,
        )

    sent = pl.ds(0, TOK_SENT)
    to_slice = [
        remote(buf, dst.at[2, :, sent], kv_send.at[i], kv_recv.at[i], other_slice)
        for i, (buf, dst) in enumerate(((ksend, kbuf), (vsend, vbuf)))
    ]
    to_core = [
        remote(buf.at[0, :, sent], buf.at[1, :, sent], kv_send.at[2 + i], kv_recv.at[2 + i], other_core)
        for i, buf in enumerate((kbuf, vbuf))
    ]
    onward = [
        remote(buf.at[2, :, sent], buf.at[3, :, sent], kv_send.at[4 + i], kv_recv.at[4 + i], other_core)
        for i, buf in enumerate((kbuf, vbuf))
    ]

    to_slice[0].start()
    for dx, dy in OFFSETS:
        remote(qbuf.at[chip], qbuf.at[chip], g_send, g_recv, device(*moved(dx, dy), core, z)).start()
    to_slice[1].start()
    to_core[0].start()
    to_core[1].start()

    lanes = lax.broadcasted_iota(jnp.int32, (GROUP, SEG), 1)
    seen = []
    for slice_ in (z, z + 1 - 2 * par):
        ok = (lanes < TOK) & (slice_ * TOK + lanes < IMG_TOK)
        seen.append(jnp.where(ok, 0.0, NEG))

    @pl.loop(0, CHIPS)
    def _(d):
        for r in range(2):
            request = 4 * d + 2 * core + r
            cited = count_ref[request]
            hit = [jnp.int32(0), jnp.int32(0)]
            for j in range(LISTS):
                slot = slot_ref[lists_ref[request, j]]
                here = jnp.where(j < cited, 1, 0)
                for i, held in enumerate((req, 2 * chip + 1 - core)):
                    hit[i] = hit[i] + jnp.where(slot == held, here, 0)
            for i in range(2):
                level = jnp.where(hit[i] > 0, 0.0, NEG)
                for s in range(2):
                    at = (2 * s + i) * SEG
                    bias[d, r * GROUP : (r + 1) * GROUP, at : at + SEG] = seen[s] + level

    to_slice[0].wait_recv()
    onward[0].start()
    to_slice[1].wait_recv()
    onward[1].start()
    wait_bytes(qbuf.at[pl.ds(0, CHIPS - 1)], g_recv)
    to_core[0].wait_recv()
    to_core[1].wait_recv()
    onward[0].wait_recv()
    onward[1].wait_recv()

    every = CHIPS * ROWS
    lane = lax.broadcasted_iota(jnp.int32, (CHIPS, GROUP, HD), 2)
    stat = jnp.zeros((CHIPS, GROUP, HD), jnp.float32)
    allowed = bias[...].reshape(every, SEGS * SEG)
    for k in range(KV_HERE):
        at = slice(k * ROWS, (k + 1) * ROWS)
        queries = qbuf[:, at, :].reshape(every, HD)
        keys = kbuf[:, k].reshape(SEGS * SEG, HD)
        values = vbuf[:, k].reshape(SEGS * SEG, HD)
        scores = lax.dot_general(
            queries, keys, (((1,), (1,)), ((), ())), preferred_element_type=jnp.float32
        )
        scores = scores * SCALE + allowed
        peak = jnp.max(scores, axis=1, keepdims=True)
        weights = jnp.exp2(scores - peak)
        total = jnp.sum(weights, axis=1, keepdims=True)
        high = weights.astype(jnp.bfloat16)
        low = (weights - high.astype(jnp.float32)).astype(jnp.bfloat16)
        weighted = jnp.dot(high, values, preferred_element_type=jnp.float32)
        weighted += jnp.dot(low, values, preferred_element_type=jnp.float32)
        obuf[:, at, :] = (weighted / total).reshape(CHIPS, ROWS, HD)
        size = (peak + jnp.log2(total)).reshape(CHIPS, 2, GROUP, 1)
        for r in range(2):
            stat = jnp.where(lane == r * KV_HERE + k, size[:, r], stat)
    obuf[:, BLOCK:, :] = stat

    for dx, dy in OFFSETS:
        x_, y_ = moved(dx, dy)
        remote(obuf.at[x_ * NY + y_], rbuf.at[chip], r_send, r_recv, device(x_, y_, core, z)).start()
    rbuf[chip] = obuf[chip]
    wait_bytes(rbuf.at[pl.ds(0, CHIPS - 1)], r_recv)

    sizes = rbuf[:, BLOCK:, :]
    largest = jnp.max(sizes, axis=0)
    share = jnp.exp2(sizes - largest[None])
    total = jnp.sum(share, axis=0)
    share = share / total[None]
    size = largest + jnp.log2(total)
    low_rows = lax.broadcasted_iota(jnp.int32, (GROUP, HD), 0) < GROUP // 2
    pl.semaphore_wait(z_ready, 2)
    for k in range(KV_HERE):
        both, logs = [], []
        for r in range(2):
            at = k * ROWS + r * GROUP
            col = r * KV_HERE + k
            part = jnp.zeros((GROUP, HD), jnp.float32)
            for s in range(CHIPS):
                part += rbuf[s, at : at + GROUP, :] * share[s, :, col : col + 1]
            both.append(part)
            logs.append(jnp.broadcast_to(size[:, col : col + 1], (GROUP, HD)))
        for h in range(2):
            for row, (a, b) in ((0, both), (GROUP, logs)):
                if h == 0:
                    tile = jnp.where(low_rows, a, pltpu.roll(b, GROUP // 2, 0))
                else:
                    tile = jnp.where(low_rows, pltpu.roll(a, GROUP // 2, 0), b)
                zsend[2 * k + h, row : row + GROUP, :] = tile
            there = 2 * (par * KV_HERE + k) + h

            @pl.when(there != z)
            def _(k=k, h=h, there=there):
                remote(
                    zsend.at[2 * k + h], zbuf.at[lax.div(z, 2)], z_send.at[2 * k + h],
                    z_recv.at[lax.div(z, 2)], device(x, y, core, there),
                ).start()

            @pl.when(there == z)
            def _(k=k, h=h):
                zbuf[lax.div(z, 2)] = zsend[2 * k + h]

    theirs = lax.div(z, NZ // 2)
    for i in range(NZ // 2):

        @pl.when(2 * i + theirs != z)
        def _(i=i):
            wait_bytes(zbuf.at[i], z_recv.at[i])

    sizes = zbuf[:, GROUP:, :]
    largest = jnp.max(sizes, axis=0)
    share = jnp.exp2(sizes - largest[None])
    out_ref[...] = jnp.sum(zbuf[:, :GROUP, :] * share, axis=0) / jnp.sum(share, axis=0)

    wait_bytes(qbuf.at[pl.ds(0, CHIPS - 1)], g_send)
    wait_bytes(rbuf.at[pl.ds(0, CHIPS - 1)], r_send)
    for copy in to_slice + to_core + onward:
        copy.wait_send()
    for i in range(NZ // 2):

        @pl.when(par * (NZ // 2) + i != z)
        def _(i=i):
            wait_bytes(zsend.at[i], z_send.at[i])


def per_device(queries, image_cache, image_lists, cited_count, image_slot):
    vmem = pl.BlockSpec(memory_space=pltpu.VMEM)
    smem = pl.BlockSpec(memory_space=pltpu.SMEM)
    block = (CHIPS, BLOCK + GROUP, HD)
    result = pl.pallas_call(
        kernel,
        name="attend",
        out_shape=jax.ShapeDtypeStruct((GROUP, HD), jnp.float32),
        in_specs=[vmem, vmem, smem, smem, smem],
        out_specs=vmem,
        scratch_shapes=[
            pltpu.VMEM((CHIPS, BLOCK, HD), jnp.bfloat16),
            pltpu.VMEM((SEGS, KV_HERE, SEG, HD), jnp.bfloat16),
            pltpu.VMEM((SEGS, KV_HERE, SEG, HD), jnp.bfloat16),
            pltpu.VMEM((KV_HERE, TOK_SENT, HD), jnp.bfloat16),
            pltpu.VMEM((KV_HERE, TOK_SENT, HD), jnp.bfloat16),
            pltpu.VMEM((CHIPS, ROWS, SEGS * SEG), jnp.float32),
            pltpu.VMEM(block, jnp.float32),
            pltpu.VMEM(block, jnp.float32),
            pltpu.VMEM((NZ // 2, 2 * GROUP, HD), jnp.float32),
            pltpu.VMEM((NZ // 2, 2 * GROUP, HD), jnp.float32),
            pltpu.SemaphoreType.DMA,
            pltpu.SemaphoreType.DMA,
            pltpu.SemaphoreType.DMA((6,)),
            pltpu.SemaphoreType.DMA((6,)),
            pltpu.SemaphoreType.DMA,
            pltpu.SemaphoreType.DMA,
            pltpu.SemaphoreType.DMA((NZ // 2,)),
            pltpu.SemaphoreType.DMA((NZ // 2,)),
            pltpu.SemaphoreType.REGULAR,
        ],
        compiler_params=pltpu.CompilerParams(
            collective_id=0, has_side_effects=True, vmem_limit_bytes=32 * 2**20
        ),
    )(queries, image_cache, image_lists, cited_count, image_slot)
    return result.reshape(2, GROUP // 2 * HD)


def solution(mesh):
    return jax.shard_map(
        per_device,
        mesh=mesh,
        in_specs=(P("req", None), P("req", "tp", None), P(), P(), P()),
        out_specs=P("req", "tp"),
        check_vma=False,
    )
```

time: 247 us -> 43.4 us (0.18)
  the two profiles are of different devices: /device:TPU:14 before, /device:TPU:1 now
where the time goes in v1:
time: 43.4 us; the launch traced here: 43.1 us
  Pallas kernels  40.7 us (94%)
  local copies, waits for them, and re-layouts  2.42 us (6%)
    pallas_call x1, Pallas kernels, per_device(): pl.pallas_call(kernel, name='attend', out_shape=jax.ShapeDtypeStruct((GRO...  40.7 us
    unnamed x9, local copies, waits for them, and re-layouts  1.82 us

profile of v1, /device:TPU:1, one launch (start us, length us, event | category | flops | bytes accessed | tf_op | source)
XLA Modules:
  0.0 43.1 jit_solution(7359287454802396496)
XLA Ops:
  0.0 0.0 copy-start.3
  0.0 0.0 copy-start.2
  0.0 0.0 copy-start.1
  0.0 0.8 %copy.6.lists_ref = s32[64,4]{1,0:T(8,128)S(1)} copy(s32[64,4]{0,1:T(4,128)} %param.7) | data formatting | bytes 2048 | tf_op args[2]
  0.8 0.0 copy-done.3
  0.8 0.0 copy-done.2
  0.8 0.0 copy-done.1
  0.8 0.0 copy-start
  0.8 1.0 %copy-done = bf16[1,104,2048]{2,1,0:T(8,128)(2,1)S(1)} copy-done((bf16[1,104,2048]{2,1,0:T(8,128)(2,1)S(1)}, bf16[1,104,2048]{2,1,0:T(8,128)(2,1)}, u32[]{:S(2)}) %copy-start) | copy-done | bytes 426008
  1.8 40.7 %attend.1 = f32[8,128]{1,0:T(8,128)S(1)} custom-call(bf16[2,8192]{1,0:T(2,128)(2,1)S(1)} %copy-done.1, bf16[1,104,2048]{2,1,0:T(8,128)(2,1)S(1)} %copy-done, s32[64,4]{1,0:T(8,128)S(1)} %copy.6.lists_ref, s32[64]{0:T(128)S(1)} %copy-done.2, s32[32]{0:T(128)S(1)} %copy-done.3), custom_call_target="tpu_custom_call" | custom-call | tf_op jit(solution)/shard_map/attend/pallas_call | solution.py:258
  42.5 0.6 %reshape.3 = f32[2,512]{1,0:T(2,128)} reshape(f32[8,128]{1,0:T(8,128)S(1)} %attend.1) | data formatting | bytes 8192 | tf_op jit(solution)/shard_map/reshape | solution.py:289
Async XLA Ops:
  0.0 0.8 %copy-start.3 = (s32[32]{0:T(128)S(1)}, s32[32]{0:T(128)}, u32[]{:S(2)}) copy-start(s32[32]{0:T(128)} %slot_ref.1) | copy-start | bytes 388
  0.0 0.8 %copy-start.2 = (s32[64]{0:T(128)S(1)}, s32[64]{0:T(128)}, u32[]{:S(2)}) copy-start(s32[64]{0:T(128)} %count_ref.1) | copy-start | bytes 772
  0.0 0.8 %copy-start.1 = (bf16[2,8192]{1,0:T(2,128)(2,1)S(1)}, bf16[2,8192]{1,0:T(2,128)(2,1)}, u32[]{:S(2)}) copy-start(bf16[2,8192]{1,0:T(2,128)(2,1)} %q_ref.1) | copy-start | bytes 98308
  0.8 1.0 %copy-start = (bf16[1,104,2048]{2,1,0:T(8,128)(2,1)S(1)}, bf16[1,104,2048]{2,1,0:T(8,128)(2,1)}, u32[]{:S(2)}) copy-start(bf16[1,104,2048]{2,1,0:T(8,128)(2,1)} %cache_ref.1) | copy-start | bytes 1277956

commit v2 on v1

v2 whole, which is shorter than its diff:
```python
import math

import jax
import jax.numpy as jnp
from jax import lax
from jax.experimental import pallas as pl
from jax.experimental.pallas import tpu as pltpu
from jax.sharding import PartitionSpec as P

KVH = 8
GROUP = 8
HD = 128
IMG_TOK = 1601
LISTS = 4
NX = 4
NY = 4
NZ = 16
CHIPS = NX * NY
REQS = 64
IMAGES = 32
TOK = 104
TOK_SENT = 112
SEG = 128
SEGS = 4
KV_HERE = KVH // 2
ROWS = 16
HALF = KV_HERE // 2 * ROWS
BLOCK = KV_HERE * ROWS
NEG = -1e30
SCALE = math.log2(math.e) / math.sqrt(HD)
MESH = pl.DeviceIdType.MESH


def wait_bytes(ref, sem):
    pltpu.make_async_copy(ref, ref, sem).wait()


def kernel(
    q_hbm, cache_hbm, lists_hbm, count_hbm, slot_hbm, out_ref,
    q_ref, cache_ref, lists_ref, count_ref, slot_ref,
    qbuf, kbuf, vbuf, ksend, vsend, bias, obuf, rbuf, zsend, zbuf,
    own_sem, g_send, g_recv, kv_send, kv_recv, r_send, r_recv, z_send, z_recv, z_near, z_far,
):
    req = lax.axis_index("req")
    z = lax.axis_index("tp")
    chip = lax.div(req, 2)
    core = lax.rem(req, 2)
    x = lax.div(chip, NY)
    y = lax.rem(chip, NY)
    par = lax.rem(z, 2)

    def device(x_, y_, c_, z_):
        return ((x_ * NY + y_) * 2 + c_, z_)

    def along_x(d):
        return lax.rem(x + d, NX)

    def along_y(d):
        return lax.rem(y + d, NY)

    def along_z(d):
        return lax.rem(z + d + NZ, NZ)

    other_core = device(x, y, 1 - core, z)
    partner = (along_z(1 - 2 * par), along_z(2 * par - 1))

    barrier = pltpu.get_barrier_semaphore()
    met = [other_core]
    met += [device(along_x(d), y, core, z) for d in (2, 1, 3)]
    met += [device(x, along_y(d), core, z) for d in (2, 1, 3)]
    met += [device(x, y, core, along_z(d)) for d in (-2, -1, 1, 2)]
    for there in met:
        pl.semaphore_signal(barrier, inc=1, device_id=there, device_id_type=MESH)

    own = [
        pltpu.make_async_copy(src, dst, own_sem.at[i])
        for i, (src, dst) in enumerate(
            (
                (q_hbm, q_ref),
                (cache_hbm, cache_ref),
                (lists_hbm, lists_ref),
                (count_hbm, count_ref),
                (slot_hbm, slot_ref),
            )
        )
    ]
    for copy in own:
        copy.start()

    own[0].wait()
    half = KV_HERE * GROUP * HD
    mine = q_ref[:, pl.ds(pl.multiple_of(par * half, half), half)].astype(jnp.float32)
    for k in range(KV_HERE):
        rows = [
            mine[r : r + 1, (k * GROUP + g) * HD : (k * GROUP + g + 1) * HD]
            for r in range(2)
            for g in range(GROUP)
        ]
        at = k % 2 * ROWS
        qbuf[x, y, k // 2, at : at + ROWS, :] = jnp.concatenate(rows, axis=0).astype(jnp.bfloat16)

    pl.semaphore_wait(barrier, len(met))
    for d in (-2, 2):
        there = device(x, y, core, along_z(d))
        pl.semaphore_signal(z_near, inc=1, device_id=there, device_id_type=MESH)

    def remote(src, dst, send, recv, there):
        return pltpu.make_async_remote_copy(
            src_ref=src, dst_ref=dst, send_sem=send, recv_sem=recv,
            device_id=there, device_id_type=MESH,
        )

    for d in (2, 1, 3):
        block = qbuf.at[x, y, 0]
        remote(block, block, g_send.at[0], g_recv.at[0], device(along_x(d), y, core, z)).start()
        block = qbuf.at[x, y, 1]
        remote(block, block, g_send.at[1], g_recv.at[1], device(x, along_y(d), core, z)).start()

    own[1].wait()
    tail = jnp.zeros((TOK_SENT - TOK, HD), jnp.bfloat16)
    sent = pl.ds(0, TOK_SENT)
    kv = ((ksend, kbuf, 0), (vsend, vbuf, KVH * HD))
    to_slice, to_core, onward = [], [], []
    for i, (outgoing, held, base) in enumerate(kv):
        for k in range(KV_HERE):
            at = pl.multiple_of(base + ((1 - par) * KV_HERE + k) * HD, HD)
            part = cache_ref[0, :, pl.ds(at, HD)]
            outgoing[k] = jnp.concatenate([part, tail], axis=0)
        for h in range(2):
            heads = pl.ds(2 * h, 2)
            to_slice.append(
                remote(
                    outgoing.at[heads], held.at[2, heads, sent], kv_send.at[4 * i + h],
                    kv_recv.at[4 * i + h], device(x, y, core, partner[h]),
                )
            )
            to_slice[-1].start()
        for k in range(KV_HERE):
            at = pl.multiple_of(base + (par * KV_HERE + k) * HD, HD)
            part = cache_ref[0, :, pl.ds(at, HD)]
            held[0, k, :TOK_SENT, :] = jnp.concatenate([part, tail], axis=0)
        to_core.append(
            remote(
                held.at[0, :, sent], held.at[1, :, sent], kv_send.at[4 * i + 2],
                kv_recv.at[4 * i + 2], other_core,
            )
        )
        to_core[-1].start()
        onward.append(
            remote(
                held.at[2, :, sent], held.at[3, :, sent], kv_send.at[4 * i + 3],
                kv_recv.at[4 * i + 3], other_core,
            )
        )

    wait_bytes(qbuf.at[pl.ds(0, NX - 1), 0, 0], g_recv.at[0])
    for d in (2, 1, 3):
        block = qbuf.at[:, y, 0]
        remote(block, block, g_send.at[2], g_recv.at[2], device(x, along_y(d), core, z)).start()
    wait_bytes(qbuf.at[0, pl.ds(0, NY - 1), 1], g_recv.at[1])
    for d in (2, 1, 3):
        block = qbuf.at[x, :, 1]
        remote(block, block, g_send.at[3], g_recv.at[3], device(along_x(d), y, core, z)).start()

    pl.semaphore_wait(z_near, 2)
    for d in (-4, 4):
        there = device(x, y, core, along_z(d))
        pl.semaphore_signal(z_far, inc=1, device_id=there, device_id_type=MESH)

    to_slice[0].wait_recv()
    to_slice[1].wait_recv()
    onward[0].start()

    pad = jnp.zeros((SEG - TOK_SENT, HD), jnp.bfloat16)
    for s in range(SEGS):
        for k in range(KV_HERE):
            kbuf[s, k, TOK_SENT:, :] = pad
            vbuf[s, k, TOK_SENT:, :] = pad

    for copy in own[2:]:
        copy.wait()
    lanes = lax.broadcasted_iota(jnp.int32, (GROUP, SEG), 1)
    seen = []
    for slice_ in (z, *partner):
        ok = (lanes < TOK) & (slice_ * TOK + lanes < IMG_TOK)
        seen.append(jnp.where(ok, 0.0, NEG))

    @pl.loop(0, CHIPS)
    def _(d):
        for r in range(2):
            request = 4 * d + 2 * core + r
            cited = count_ref[request]
            hit = [jnp.int32(0), jnp.int32(0)]
            for j in range(LISTS):
                slot = slot_ref[lists_ref[j, request]]
                here = jnp.where(j < cited, 1, 0)
                for i, stored in enumerate((req, 2 * chip + 1 - core)):
                    hit[i] = hit[i] + jnp.where(slot == stored, here, 0)
            for i in range(2):
                level = jnp.where(hit[i] > 0, 0.0, NEG)
                for s in range(3):
                    at = (2 * s + i) * SEG
                    bias[lax.div(d, NY), lax.rem(d, NY), r * GROUP : (r + 1) * GROUP, at : at + SEG] = seen[s] + level

    to_slice[2].wait_recv()
    to_slice[3].wait_recv()
    onward[1].start()
    wait_bytes(qbuf.at[:, pl.ds(0, NY - 1), 0], g_recv.at[2])
    wait_bytes(qbuf.at[pl.ds(0, NX - 1), :, 1], g_recv.at[3])
    to_core[0].wait_recv()
    onward[0].wait_recv()

    some = 2 * NY
    lane = lax.broadcasted_iota(jnp.int32, (some, GROUP, HD), 2)
    for part in range(2):
        columns = (along_x(2), along_x(1)) if part == 0 else (along_x(3), x)
        levels = jnp.concatenate([bias[c].reshape(NY * ROWS, 6 * SEG) for c in columns], axis=0)
        softmax = []
        for k in range(KV_HERE):
            at = slice(k % 2 * ROWS, (k % 2 + 1) * ROWS)
            queries = jnp.concatenate(
                [qbuf[c, :, k // 2, at, :].reshape(NY * ROWS, HD) for c in columns], axis=0
            )
            keys = kbuf[:, k].reshape(SEGS * SEG, HD)
            scores = lax.dot_general(
                queries, keys, (((1,), (1,)), ((), ())), preferred_element_type=jnp.float32
            )
            near = levels[:, : 2 * SEG]
            far = levels[:, (2 + 2 * (k // 2)) * SEG : (4 + 2 * (k // 2)) * SEG]
            scores = scores * SCALE + jnp.concatenate([near, far], axis=1)
            peak = jnp.max(scores, axis=1, keepdims=True)
            weights = jnp.exp2(scores - peak)
            total = jnp.sum(weights, axis=1, keepdims=True)
            high = weights.astype(jnp.bfloat16)
            low = (weights - high.astype(jnp.float32)).astype(jnp.bfloat16)
            softmax.append((high, low, peak, total))
        if part == 0:
            to_core[1].wait_recv()
            onward[1].wait_recv()
        stat = jnp.zeros((some, GROUP, HD), jnp.float32)
        for k in range(KV_HERE):
            high, low, peak, total = softmax[k]
            values = vbuf[:, k].reshape(SEGS * SEG, HD)
            weighted = jnp.dot(high, values, preferred_element_type=jnp.float32)
            weighted += jnp.dot(low, values, preferred_element_type=jnp.float32)
            weighted = (weighted / total).reshape(2, NY, ROWS, HD)
            for i, c in enumerate(columns):
                obuf[pl.ds(c * NY, NY), k * ROWS : (k + 1) * ROWS, :] = weighted[i]
            size = (peak + jnp.log2(total)).reshape(some, 2, GROUP, 1)
            for r in range(2):
                stat = jnp.where(lane == r * KV_HERE + k, size[:, r], stat)
        for i, c in enumerate(columns):
            obuf[pl.ds(c * NY, NY), BLOCK:, :] = stat[i * NY : (i + 1) * NY]
        for i, c in enumerate(columns):
            for d in (2, 1, 3, 0):
                if part == 1 and i == 1 and d == 0:
                    continue
                row = along_y(d)
                remote(obuf.at[c * NY + row], rbuf.at[chip], r_send, r_recv, device(c, row, core, z)).start()
    rbuf[chip] = obuf[chip]
    pl.semaphore_wait(z_far, 2)
    wait_bytes(rbuf.at[pl.ds(0, CHIPS - 1)], r_recv)

    sizes = rbuf[:, BLOCK:, :]
    largest = jnp.max(sizes, axis=0)
    share = jnp.exp2(sizes - largest[None])
    total = jnp.sum(share, axis=0)
    share = share / total[None]
    size = largest + jnp.log2(total)
    low_rows = lax.broadcasted_iota(jnp.int32, (GROUP, HD), 0) < GROUP // 2
    for k in range(KV_HERE):
        both, logs = [], []
        for r in range(2):
            at = k * ROWS + r * GROUP
            col = r * KV_HERE + k
            result = jnp.zeros((GROUP, HD), jnp.float32)
            for s in range(CHIPS):
                result += rbuf[s, at : at + GROUP, :] * share[s, :, col : col + 1]
            both.append(result)
            logs.append(jnp.broadcast_to(size[:, col : col + 1], (GROUP, HD)))
        for h in range(2):
            for row, (a, b) in ((0, both), (GROUP, logs)):
                if h == 0:
                    tile = jnp.where(low_rows, a, pltpu.roll(b, GROUP // 2, 0))
                else:
                    tile = jnp.where(low_rows, pltpu.roll(a, GROUP // 2, 0), b)
                zsend[2 * k + h, row : row + GROUP, :] = tile
            there = 2 * (par * KV_HERE + k) + h

            @pl.when(there != z)
            def _(k=k, h=h, there=there):
                remote(
                    zsend.at[2 * k + h], zbuf.at[lax.div(z, 2)], z_send.at[2 * k + h],
                    z_recv.at[lax.div(z, 2)], device(x, y, core, there),
                ).start()

            @pl.when(there == z)
            def _(k=k, h=h):
                zbuf[lax.div(z, 2)] = zsend[2 * k + h]

    theirs = lax.div(z, NZ // 2)
    for i in range(NZ // 2):

        @pl.when(2 * i + theirs != z)
        def _(i=i):
            wait_bytes(zbuf.at[i], z_recv.at[i])

    sizes = zbuf[:, GROUP:, :]
    largest = jnp.max(sizes, axis=0)
    share = jnp.exp2(sizes - largest[None])
    out_ref[...] = jnp.sum(zbuf[:, :GROUP, :] * share, axis=0) / jnp.sum(share, axis=0)

    wait_bytes(qbuf.at[pl.ds(0, NX - 1), 0, 0], g_send.at[0])
    wait_bytes(qbuf.at[0, pl.ds(0, NY - 1), 1], g_send.at[1])
    wait_bytes(qbuf.at[:, pl.ds(0, NY - 1), 0], g_send.at[2])
    wait_bytes(qbuf.at[pl.ds(0, NX - 1), :, 1], g_send.at[3])
    wait_bytes(rbuf.at[pl.ds(0, CHIPS - 1)], r_send)
    for copy in to_slice + to_core + onward:
        copy.wait_send()
    for i in range(NZ // 2):

        @pl.when(par * (NZ // 2) + i != z)
        def _(i=i):
            wait_bytes(zsend.at[i], z_send.at[i])


def per_device(queries, image_cache, image_lists, cited_count, image_slot):
    here = pl.BlockSpec(memory_space=pl.ANY)
    block = (CHIPS, BLOCK + GROUP, HD)
    held = (SEGS, KV_HERE, SEG, HD)
    result = pl.pallas_call(
        kernel,
        name="attend",
        out_shape=jax.ShapeDtypeStruct((GROUP, HD), jnp.float32),
        in_specs=[here] * 5,
        out_specs=pl.BlockSpec(memory_space=pltpu.VMEM),
        scratch_shapes=[
            pltpu.VMEM(queries.shape, jnp.bfloat16),
            pltpu.VMEM(image_cache.shape, jnp.bfloat16),
            pltpu.SMEM((LISTS, REQS), jnp.int32),
            pltpu.SMEM((REQS,), jnp.int32),
            pltpu.SMEM((IMAGES,), jnp.int32),
            pltpu.VMEM((NX, NY, 2, HALF, HD), jnp.bfloat16),
            pltpu.VMEM(held, jnp.bfloat16),
            pltpu.VMEM(held, jnp.bfloat16),
            pltpu.VMEM((KV_HERE, TOK_SENT, HD), jnp.bfloat16),
            pltpu.VMEM((KV_HERE, TOK_SENT, HD), jnp.bfloat16),
            pltpu.VMEM((NX, NY, ROWS, 6 * SEG), jnp.float32),
            pltpu.VMEM(block, jnp.float32),
            pltpu.VMEM(block, jnp.float32),
            pltpu.VMEM((NZ // 2, 2 * GROUP, HD), jnp.float32),
            pltpu.VMEM((NZ // 2, 2 * GROUP, HD), jnp.float32),
            pltpu.SemaphoreType.DMA((5,)),
            pltpu.SemaphoreType.DMA((4,)),
            pltpu.SemaphoreType.DMA((4,)),
            pltpu.SemaphoreType.DMA((8,)),
            pltpu.SemaphoreType.DMA((8,)),
            pltpu.SemaphoreType.DMA,
            pltpu.SemaphoreType.DMA,
            pltpu.SemaphoreType.DMA((NZ // 2,)),
            pltpu.SemaphoreType.DMA((NZ // 2,)),
            pltpu.SemaphoreType.REGULAR,
            pltpu.SemaphoreType.REGULAR,
        ],
        compiler_params=pltpu.CompilerParams(
            collective_id=0, has_side_effects=True, vmem_limit_bytes=60 * 2**20
        ),
    )(queries, image_cache, image_lists.T, cited_count, image_slot)
    return result.reshape(2, GROUP // 2 * HD)


def solution(mesh):
    return jax.shard_map(
        per_device,
        mesh=mesh,
        in_specs=(P("req", None), P("req", "tp", None), P(), P(), P()),
        out_specs=P("req", "tp"),
        check_vma=False,
    )
```

time: 43.4 us -> 38.9 us (0.90)
  the two profiles are of different devices: /device:TPU:1 before, /device:TPU:2 now
where the time goes in v2:
time: 38.9 us; the launch traced here: 38.8 us
  Pallas kernels  37.5 us (96%)
  local copies, waits for them, and re-layouts  1.28 us (3%)
    pallas_call x1, Pallas kernels, per_device(): pl.pallas_call(kernel, name='attend', out_shape=jax.ShapeDtypeStruct((GRO...  37.5 us
    reshape x1, local copies, waits for them, and re-layouts, per_device(): return result.reshape(2, GROUP // 2 * HD)  1.28 us

profile of v2, /device:TPU:2, one launch (start us, length us, event | category | flops | bytes accessed | tf_op | source)
XLA Modules:
  0.0 38.8 jit_solution(15032860473048919504)
XLA Ops:
  0.0 37.5 %attend.1 = f32[8,128]{1,0:T(8,128)} custom-call(bf16[2,8192]{1,0:T(2,128)(2,1)} %q_hbm.1, bf16[1,104,2048]{2,1,0:T(8,128)(2,1)} %cache_hbm.1, s32[4,64]{1,0:T(4,128)} %bitcast.1, s32[64]{0:T(128)} %count_hbm.1, s32[32]{0:T(128)} %slot_hbm.1), custom_call_target="tpu_custom_call" | custom-call | tf_op jit(solution)/shard_map/attend/pallas_call | solution.py:331
  37.5 1.3 %reshape.3 = f32[2,512]{1,0:T(2,128)} reshape(f32[8,128]{1,0:T(8,128)} %attend.1) | data formatting | bytes 8192 | tf_op jit(solution)/shard_map/reshape | solution.py:369

commit v3 on v2

v3 whole, which is shorter than its diff:
```python
import math

import jax
import jax.numpy as jnp
from jax import lax
from jax.experimental import pallas as pl
from jax.experimental.pallas import tpu as pltpu
from jax.sharding import PartitionSpec as P

KVH = 8
GROUP = 8
HD = 128
IMG_TOK = 1601
LISTS = 4
NX = 4
NY = 4
NZ = 16
CHIPS = NX * NY
REQS = 64
IMAGES = 32
TOK = 104
TOK_SENT = 112
SEG = 128
SEGS = 4
KV_HERE = KVH // 2
ROWS = 16
NEG = -1e30
SCALE = math.log2(math.e) / math.sqrt(HD)
MESH = pl.DeviceIdType.MESH


def wait_bytes(ref, sem):
    pltpu.make_async_copy(ref, ref, sem).wait()


def kernel(
    q_hbm, cache_hbm, lists_hbm, count_hbm, slot_hbm, out_ref,
    q_ref, cache_ref, lists_ref, count_ref, slot_ref,
    qbuf, kvbuf, kvsend, bias, first_out, first_in, rest_out, rest_in, zsend, zbuf,
    own_sem, q_send, q_recv, kv_send, kv_recv, r_send, r_recv, z_send, z_recv, z_near, z_far,
):
    req = lax.axis_index("req")
    z = lax.axis_index("tp")
    chip = lax.div(req, 2)
    core = lax.rem(req, 2)
    x = lax.div(chip, NY)
    y = lax.rem(chip, NY)
    par = lax.rem(z, 2)

    def device(x_, y_, c_, z_):
        return ((x_ * NY + y_) * 2 + c_, z_)

    def along_x(d):
        return lax.rem(x + d, NX)

    def along_y(d):
        return lax.rem(y + d, NY)

    def along_z(d):
        return lax.rem(z + d + NZ, NZ)

    other_core = device(x, y, 1 - core, z)
    partner = (along_z(1 - 2 * par), along_z(2 * par - 1))

    def key_head(k, par_):
        return 2 * k + 1 - par_

    barrier = pltpu.get_barrier_semaphore()
    met = [device(along_x(d), y, core, z) for d in (2, 1, 3)]
    met += [device(x, along_y(d), core, z) for d in (2, 1, 3)]
    met += [device(x, y, core, along_z(d)) for d in (-2, -1, 1, 2)]
    met += [other_core]
    for there in met:
        pl.semaphore_signal(barrier, inc=1, device_id=there, device_id_type=MESH)

    own = [
        pltpu.make_async_copy(src, dst, own_sem.at[i])
        for i, (src, dst) in enumerate(
            (
                (q_hbm, q_ref),
                (cache_hbm, cache_ref),
                (lists_hbm, lists_ref),
                (count_hbm, count_ref),
                (slot_hbm, slot_ref),
            )
        )
    ]
    for copy in own:
        copy.start()

    own[0].wait()
    for k in range(KV_HERE):
        width = GROUP * HD
        at = pl.multiple_of(key_head(k, par) * width, width)
        mine = q_ref[:, pl.ds(at, width)].astype(jnp.float32)
        rows = [mine[r : r + 1, g * HD : (g + 1) * HD] for r in range(2) for g in range(GROUP)]
        qbuf[x, y, k] = jnp.concatenate(rows, axis=0).astype(jnp.bfloat16)

    pl.semaphore_wait(barrier, len(met))

    def remote(src, dst, send, recv, there):
        return pltpu.make_async_remote_copy(
            src_ref=src, dst_ref=dst, send_sem=send, recv_sem=recv,
            device_id=there, device_id_type=MESH,
        )

    rest = pl.ds(1, KV_HERE - 1)
    for d in (2, 1, 3):
        block = qbuf.at[x, y, 0]
        remote(block, block, q_send.at[0], q_recv.at[0], device(along_x(d), y, core, z)).start()
    for d in (2, 1, 3):
        block = qbuf.at[x, y, rest]
        remote(block, block, q_send.at[1], q_recv.at[1], device(x, along_y(d), core, z)).start()

    for d in (-2, 2):
        there = device(x, y, core, along_z(d))
        pl.semaphore_signal(z_near, inc=1, device_id=there, device_id_type=MESH)

    own[1].wait()
    tail = jnp.zeros((TOK_SENT - TOK, HD), jnp.bfloat16)
    sent = pl.ds(0, TOK_SENT)

    def stored(k, par_, i):
        at = pl.multiple_of((i * KVH + key_head(k, par_)) * HD, HD)
        return jnp.concatenate([cache_ref[0, :, pl.ds(at, HD)], tail], axis=0)

    def kv_copy(i, src, dst, there):
        return remote(src, dst, kv_send.at[i], kv_recv.at[i], there)

    neighbour = [device(x, y, core, partner[h]) for h in range(2)]
    late = pl.ds(2, 2)
    to_slice = [
        kv_copy(0, kvsend.at[0, 0], kvbuf.at[2, 0, 0, sent], neighbour[0]),
        kv_copy(1, kvsend.at[0, 1], kvbuf.at[2, 0, 1, sent], neighbour[0]),
        kv_copy(2, kvsend.at[1], kvbuf.at[2, 1, :, sent], neighbour[0]),
        kv_copy(3, kvsend.at[late], kvbuf.at[2, late, :, sent], neighbour[1]),
    ]
    to_core = [
        kv_copy(4, kvbuf.at[0, 0, 0, sent], kvbuf.at[1, 0, 0, sent], other_core),
        kv_copy(5, kvbuf.at[0, 0, 1, sent], kvbuf.at[1, 0, 1, sent], other_core),
        kv_copy(6, kvbuf.at[0, rest, :, sent], kvbuf.at[1, rest, :, sent], other_core),
    ]
    onward = [
        kv_copy(7, kvbuf.at[2, 0, 0, sent], kvbuf.at[3, 0, 0, sent], other_core),
        kv_copy(8, kvbuf.at[2, 0, 1, sent], kvbuf.at[3, 0, 1, sent], other_core),
        kv_copy(9, kvbuf.at[2, 1, :, sent], kvbuf.at[3, 1, :, sent], other_core),
        kv_copy(10, kvbuf.at[2, late, :, sent], kvbuf.at[3, late, :, sent], other_core),
    ]
    for i in range(2):
        kvsend[0, i] = stored(0, 1 - par, i)
        to_slice[i].start()
    for i in range(2):
        kvbuf[0, 0, i, :TOK_SENT, :] = stored(0, par, i)
        to_core[i].start()
    for k in range(1, KV_HERE):
        for i in range(2):
            kvsend[k, i] = stored(k, 1 - par, i)
    to_slice[2].start()
    to_slice[3].start()
    for k in range(1, KV_HERE):
        for i in range(2):
            kvbuf[0, k, i, :TOK_SENT, :] = stored(k, par, i)
    to_core[2].start()

    pad = jnp.zeros((SEG - TOK_SENT, HD), jnp.bfloat16)
    for s in range(SEGS):
        for k in range(KV_HERE):
            for i in range(2):
                kvbuf[s, k, i, TOK_SENT:, :] = pad

    for copy in own[2:]:
        copy.wait()
    lanes = lax.broadcasted_iota(jnp.int32, (GROUP, SEG), 1)
    seen = []
    for slice_ in (z, *partner):
        ok = (lanes < TOK) & (slice_ * TOK + lanes < IMG_TOK)
        seen.append(jnp.where(ok, 0.0, NEG))

    @pl.loop(0, CHIPS)
    def _(d):
        for r in range(2):
            request = 4 * d + 2 * core + r
            cited = count_ref[request]
            hit = [jnp.int32(0), jnp.int32(0)]
            for j in range(LISTS):
                slot = slot_ref[lists_ref[j, request]]
                here = jnp.where(j < cited, 1, 0)
                for i, stored_here in enumerate((req, 2 * chip + 1 - core)):
                    hit[i] = hit[i] + jnp.where(slot == stored_here, here, 0)
            for i in range(2):
                level = jnp.where(hit[i] > 0, 0.0, NEG)
                for s in range(3):
                    at = (2 * s + i) * SEG
                    bias[d, r * GROUP : (r + 1) * GROUP, at : at + SEG] = seen[s] + level

    wait_bytes(qbuf.at[pl.ds(0, NX - 1), 0, 0], q_recv.at[0])
    for d in (2, 1, 3):
        block = qbuf.at[:, y, 0]
        remote(block, block, q_send.at[2], q_recv.at[2], device(x, along_y(d), core, z)).start()
    wait_bytes(qbuf.at[0, pl.ds(0, NY - 1), rest], q_recv.at[1])
    for d in (2, 1, 3):
        block = qbuf.at[x, :, rest]
        remote(block, block, q_send.at[3], q_recv.at[3], device(along_x(d), y, core, z)).start()

    for i in range(2):
        to_slice[i].wait_recv()
        onward[i].start()

    pl.semaphore_wait(z_near, 2)
    for d in (-4, 4):
        there = device(x, y, core, along_z(d))
        pl.semaphore_signal(z_far, inc=1, device_id=there, device_id_type=MESH)

    def scored(k, columns):
        queries = jnp.concatenate([qbuf[c, :, k].reshape(NY * ROWS, HD) for c in columns], axis=0)
        keys = kvbuf[:, k, 0].reshape(SEGS * SEG, HD)
        scores = lax.dot_general(
            queries, keys, (((1,), (1,)), ((), ())), preferred_element_type=jnp.float32
        )
        far = (2 + 2 * (k // 2)) * SEG
        allowed = [
            jnp.concatenate(
                [bias[pl.ds(c * NY, NY), :, : 2 * SEG], bias[pl.ds(c * NY, NY), :, far : far + 2 * SEG]],
                axis=2,
            ).reshape(NY * ROWS, SEGS * SEG)
            for c in columns
        ]
        scores = scores * SCALE + jnp.concatenate(allowed, axis=0)
        peak = jnp.max(scores, axis=1, keepdims=True)
        weights = jnp.exp2(scores - peak)
        total = jnp.sum(weights, axis=1, keepdims=True)
        high = weights.astype(jnp.bfloat16)
        low = (weights - high.astype(jnp.float32)).astype(jnp.bfloat16)
        return high, low, peak, total

    def weigh(ks, columns, softmax, out):
        some = len(columns) * NY
        lane = lax.broadcasted_iota(jnp.int32, (some, GROUP, HD), 2)
        stat = jnp.zeros((some, GROUP, HD), jnp.float32)
        for n, k in enumerate(ks):
            high, low, peak, total = softmax[n]
            values = kvbuf[:, k, 1].reshape(SEGS * SEG, HD)
            weighted = jnp.dot(high, values, preferred_element_type=jnp.float32)
            weighted += jnp.dot(low, values, preferred_element_type=jnp.float32)
            weighted = (weighted / total).reshape(some, ROWS, HD)
            for i, c in enumerate(columns):
                out[pl.ds(c * NY, NY), n * ROWS : (n + 1) * ROWS, :] = weighted[i * NY : (i + 1) * NY]
            size = (peak + jnp.log2(total)).reshape(some, 2, GROUP, 1)
            for r in range(2):
                stat = jnp.where(lane == r * len(ks) + n, size[:, r], stat)
        for i, c in enumerate(columns):
            out[pl.ds(c * NY, NY), len(ks) * ROWS :, :] = stat[i * NY : (i + 1) * NY]

    def go_home(columns, out, arrived, i):
        for c, skip in columns:
            for d in (2, 1, 3) if skip else (2, 1, 3, 0):
                row = along_y(d)
                there = device(c, row, core, z)
                remote(out.at[c * NY + row], arrived.at[chip], r_send.at[i], r_recv.at[i], there).start()

    far_columns, near_columns = [along_x(2), along_x(1)], [along_x(3), x]
    wait_bytes(qbuf.at[:, pl.ds(0, NY - 1), 0], q_recv.at[2])
    to_core[0].wait_recv()
    onward[0].wait_recv()
    softmax = [scored(0, columns) for columns in (far_columns, near_columns)]
    to_core[1].wait_recv()
    onward[1].wait_recv()
    weigh([0], far_columns, softmax[:1], first_out)
    go_home([(c, False) for c in far_columns], first_out, first_in, 0)
    weigh([0], near_columns, softmax[1:], first_out)
    go_home([(near_columns[0], False), (x, True)], first_out, first_in, 0)
    first_in[chip] = first_out[chip]

    for i in range(2, 4):
        to_slice[i].wait_recv()
        onward[i].start()
    wait_bytes(qbuf.at[pl.ds(0, NX - 1), :, rest], q_recv.at[3])
    to_core[2].wait_recv()
    onward[2].wait_recv()
    onward[3].wait_recv()
    later = list(range(1, KV_HERE))
    for columns in (far_columns, near_columns):
        weigh(later, columns, [scored(k, columns) for k in later], rest_out)
        go_home([(columns[0], False), (columns[1], columns is near_columns)], rest_out, rest_in, 1)
    rest_in[chip] = rest_out[chip]

    low_rows = lax.broadcasted_iota(jnp.int32, (GROUP, HD), 0) < GROUP // 2

    def spread(ks, arrived):
        data = len(ks) * ROWS
        sizes = arrived[:, data:, :]
        largest = jnp.max(sizes, axis=0)
        share = jnp.exp2(sizes - largest[None])
        total = jnp.sum(share, axis=0)
        share = share / total[None]
        size = largest + jnp.log2(total)
        for n, k in enumerate(ks):
            both, logs = [], []
            for r in range(2):
                at = n * ROWS + r * GROUP
                col = r * len(ks) + n
                parts = [arrived[s, at : at + GROUP, :] * share[s, :, col : col + 1] for s in range(CHIPS)]
                while len(parts) > 1:
                    parts = [a + b for a, b in zip(parts[::2], parts[1::2])]
                both.append(parts[0])
                logs.append(jnp.broadcast_to(size[:, col : col + 1], (GROUP, HD)))
            for h in range(2):
                for row, (a, b) in ((0, both), (GROUP, logs)):
                    if h == 0:
                        tile = jnp.where(low_rows, a, pltpu.roll(b, GROUP // 2, 0))
                    else:
                        tile = jnp.where(low_rows, pltpu.roll(a, GROUP // 2, 0), b)
                    zsend[2 * k + h, row : row + GROUP, :] = tile
                there = 2 * key_head(k, par) + h

                @pl.when(there != z)
                def _():
                    remote(
                        zsend.at[2 * k + h], zbuf.at[lax.div(z, 2)], z_send.at[2 * k + h],
                        z_recv.at[lax.div(z, 2)], device(x, y, core, there),
                    ).start()

                @pl.when(there == z)
                def _():
                    zbuf[lax.div(z, 2)] = zsend[2 * k + h]

    pl.semaphore_wait(z_far, 2)
    wait_bytes(first_in.at[pl.ds(0, CHIPS - 1)], r_recv.at[0])
    spread([0], first_in)
    wait_bytes(rest_in.at[pl.ds(0, CHIPS - 1)], r_recv.at[1])
    spread(later, rest_in)

    theirs = 1 - lax.rem(lax.div(z, 2), 2)
    for i in range(NZ // 2):

        @pl.when(2 * i + theirs != z)
        def _(i=i):
            wait_bytes(zbuf.at[i], z_recv.at[i])

    sizes = zbuf[:, GROUP:, :]
    largest = jnp.max(sizes, axis=0)
    share = jnp.exp2(sizes - largest[None])
    out_ref[...] = jnp.sum(zbuf[:, :GROUP, :] * share, axis=0) / jnp.sum(share, axis=0)

    wait_bytes(qbuf.at[pl.ds(0, NX - 1), 0, 0], q_send.at[0])
    wait_bytes(qbuf.at[0, pl.ds(0, NY - 1), rest], q_send.at[1])
    wait_bytes(qbuf.at[:, pl.ds(0, NY - 1), 0], q_send.at[2])
    wait_bytes(qbuf.at[pl.ds(0, NX - 1), :, rest], q_send.at[3])
    wait_bytes(first_in.at[pl.ds(0, CHIPS - 1)], r_send.at[0])
    wait_bytes(rest_in.at[pl.ds(0, CHIPS - 1)], r_send.at[1])
    for copy in to_slice + to_core + onward:
        copy.wait_send()
    for k in range(KV_HERE):
        for h in range(2):

            @pl.when(2 * key_head(k, par) + h != z)
            def _():
                wait_bytes(zsend.at[2 * k + h], z_send.at[2 * k + h])


def per_device(queries, image_cache, image_lists, cited_count, image_slot):
    here = pl.BlockSpec(memory_space=pl.ANY)
    first = (CHIPS, ROWS + GROUP, HD)
    rest = (CHIPS, (KV_HERE - 1) * ROWS + GROUP, HD)
    result = pl.pallas_call(
        kernel,
        name="attend",
        out_shape=jax.ShapeDtypeStruct((GROUP, HD), jnp.float32),
        in_specs=[here] * 5,
        out_specs=pl.BlockSpec(memory_space=pltpu.VMEM),
        scratch_shapes=[
            pltpu.VMEM(queries.shape, jnp.bfloat16),
            pltpu.VMEM(image_cache.shape, jnp.bfloat16),
            pltpu.SMEM((LISTS, REQS), jnp.int32),
            pltpu.SMEM((REQS,), jnp.int32),
            pltpu.SMEM((IMAGES,), jnp.int32),
            pltpu.VMEM((NX, NY, KV_HERE, ROWS, HD), jnp.bfloat16),
            pltpu.VMEM((SEGS, KV_HERE, 2, SEG, HD), jnp.bfloat16),
            pltpu.VMEM((KV_HERE, 2, TOK_SENT, HD), jnp.bfloat16),
            pltpu.VMEM((CHIPS, ROWS, 6 * SEG), jnp.float32),
            pltpu.VMEM(first, jnp.float32),
            pltpu.VMEM(first, jnp.float32),
            pltpu.VMEM(rest, jnp.float32),
            pltpu.VMEM(rest, jnp.float32),
            pltpu.VMEM((NZ // 2, 2 * GROUP, HD), jnp.float32),
            pltpu.VMEM((NZ // 2, 2 * GROUP, HD), jnp.float32),
            pltpu.SemaphoreType.DMA((5,)),
            pltpu.SemaphoreType.DMA((4,)),
            pltpu.SemaphoreType.DMA((4,)),
            pltpu.SemaphoreType.DMA((11,)),
            pltpu.SemaphoreType.DMA((11,)),
            pltpu.SemaphoreType.DMA((2,)),
            pltpu.SemaphoreType.DMA((2,)),
            pltpu.SemaphoreType.DMA((NZ // 2,)),
            pltpu.SemaphoreType.DMA((NZ // 2,)),
            pltpu.SemaphoreType.REGULAR,
            pltpu.SemaphoreType.REGULAR,
        ],
        compiler_params=pltpu.CompilerParams(
            collective_id=0, has_side_effects=True, vmem_limit_bytes=60 * 2**20
        ),
    )(queries, image_cache, image_lists.T, cited_count, image_slot)
    return result.reshape(2, GROUP // 2 * HD)


def solution(mesh):
    return jax.shard_map(
        per_device,
        mesh=mesh,
        in_specs=(P("req", None), P("req", "tp", None), P(), P(), P()),
        out_specs=P("req", "tp"),
        check_vma=False,
    )
```

time: 38.9 us -> 35.6 us (0.915)
  the two profiles are of different devices: /device:TPU:2 before, /device:TPU:1 now
where the time goes in v3:
time: 35.6 us; the launch traced here: 35 us
  Pallas kernels  33.7 us (95%)
  local copies, waits for them, and re-layouts  1.28 us (4%)
    pallas_call x1, Pallas kernels, per_device(): pl.pallas_call(kernel, name='attend', out_shape=jax.ShapeDtypeStruct((GRO...  33.7 us
    reshape x1, local copies, waits for them, and re-layouts, per_device(): return result.reshape(2, GROUP // 2 * HD)  1.28 us

profile of v3, /device:TPU:1, one launch (start us, length us, event | category | flops | bytes accessed | tf_op | source)
XLA Modules:
  0.0 35.0 jit_solution(14866822749117824743)
XLA Ops:
  0.0 33.7 %attend.1 = f32[8,128]{1,0:T(8,128)} custom-call(bf16[2,8192]{1,0:T(2,128)(2,1)} %q_hbm.1, bf16[1,104,2048]{2,1,0:T(8,128)(2,1)} %cache_hbm.1, s32[4,64]{1,0:T(4,128)} %bitcast.1, s32[64]{0:T(128)} %count_hbm.1, s32[32]{0:T(128)} %slot_hbm.1), custom_call_target="tpu_custom_call" | custom-call | tf_op jit(solution)/shard_map/attend/pallas_call | solution.py:365
  33.7 1.3 %reshape.3 = f32[2,512]{1,0:T(2,128)} reshape(f32[8,128]{1,0:T(8,128)} %attend.1) | data formatting | bytes 8192 | tf_op jit(solution)/shard_map/reshape | solution.py:403

commit v4 on v0

v4 whole, which is shorter than its diff:
```python
import math

import jax
import jax.numpy as jnp
from jax import lax
from jax.experimental import pallas as pl
from jax.experimental.pallas import tpu as pltpu
from jax.sharding import PartitionSpec as P

KVH = 8
GROUP = 8
HD = 128
IMG_TOK = 1601
LISTS = 4
SIDE = 4
NZ = 16
REQS = 64
IMAGES = 32
TOK = 104
TOK_SENT = 112
SEG = 128
LINE = 2 * SIDE
ROWS = 16
STAGES = KVH // 2
PAIRS = (0, 1, 3, 2)
NEG = -1e30
SCALE = math.log2(math.e) / math.sqrt(HD)
MESH = pl.DeviceIdType.MESH
FIRST_LATE = NZ // 2
GREETED = tuple(min(n, 8) if n < 12 else 7 if n == 12 else 6 for n in range(NZ))


def wait_bytes(ref, sem):
    pltpu.make_async_copy(ref, ref, sem).wait()


def kernel(
    q_hbm, cache_hbm, lists_hbm, count_hbm, slot_hbm, out_ref,
    q_ref, cache_ref, lists_ref, count_ref, slot_ref,
    q_own, kv_own, q_buf, kv_buf, bias, home_out, home_in, z_out, z_in,
    own_sem, q_send, q_recv, kv_send, kv_recv, h_send, h_recv, z_send, z_recv, z_met,
):
    req = lax.axis_index("req")
    z = lax.axis_index("tp")
    core = lax.rem(req, 2)
    x = lax.div(req, 2 * SIDE)
    y = lax.rem(lax.div(req, 2), SIDE)
    even = core == 0

    def device(x_, y_, c_, z_=z):
        return ((x_ * SIDE + y_) * 2 + c_, z_)

    def along_x(d, c_):
        return device(lax.rem(x + d, SIDE), y, c_)

    def along_y(d, c_):
        return device(x, lax.rem(y + d, SIDE), c_)

    def along_z(d):
        return device(x, y, core, lax.rem(z + d + NZ, NZ))

    other_core = device(x, y, 1 - core)
    kv_place = jnp.where(even, x, y)
    q_place = jnp.where(even, y, x)

    barrier = pltpu.get_barrier_semaphore()
    met = [line(d, c_) for d in (2, 1, 3) for line in (along_x, along_y) for c_ in range(2)]
    met += [other_core]
    for there in met:
        pl.semaphore_signal(barrier, inc=1, device_id=there, device_id_type=MESH)
    late = z >= FIRST_LATE

    def near(d):
        return late & (z + d >= FIRST_LATE) & (z + d < NZ)

    for d in (-2, -1, 1, 2):

        @pl.when(near(d))
        def _():
            pl.semaphore_signal(barrier, inc=1, device_id=along_z(d), device_id_type=MESH)

    for n in range(NZ - 1, 0, -1):

        @pl.when(z < GREETED[n])
        def _():
            there = device(x, y, core, n)
            pl.semaphore_signal(barrier, inc=1, device_id=there, device_id_type=MESH)

    own = [
        pltpu.make_async_copy(src, dst, own_sem.at[i])
        for i, (src, dst) in enumerate(
            (
                (q_hbm, q_ref),
                (cache_hbm, cache_ref),
                (lists_hbm, lists_ref),
                (count_hbm, count_ref),
                (slot_hbm, slot_ref),
            )
        )
    ]
    for copy in own:
        copy.start()

    own[0].wait()
    for s in range(STAGES):
        for c in range(2):
            first = (2 * PAIRS[s] + c) * GROUP * HD
            mine = q_ref[:, first : first + GROUP * HD].astype(jnp.float32)
            rows = [mine[r : r + 1, g * HD : (g + 1) * HD] for r in range(2) for g in range(GROUP)]
            q_own[c, s] = jnp.concatenate(rows, axis=0).astype(jnp.bfloat16)
    q_buf[2 * q_place + core] = q_own[core]

    own[1].wait()
    tail = jnp.zeros((TOK_SENT - TOK, HD), jnp.bfloat16)
    for k in range(KVH):
        for i in range(2):
            first = (i * KVH + k) * HD
            kv_own[k, i] = jnp.concatenate([cache_ref[0, :, first : first + HD], tail], axis=0)
    pad = jnp.zeros((SEG - TOK_SENT, HD), jnp.bfloat16)
    for s in range(STAGES):
        kv_buf[s, 2 * kv_place + core, :, :TOK_SENT, :] = kv_own[2 * PAIRS[s] + core]
        for n in range(LINE):
            for i in range(2):
                kv_buf[s, n, i, TOK_SENT:, :] = pad

    greeted = jnp.int32(len(met))
    for d in (-2, -1, 1, 2):
        greeted = greeted + jnp.where(near(d), 1, 0)
    for n in range(1, NZ):
        greeted = greeted + jnp.where(z == n, GREETED[n], 0)
    pl.semaphore_wait(barrier, greeted)

    def send(src, dst, sems, n, there):
        send_sem, recv_sem = sems
        pltpu.make_async_remote_copy(
            src_ref=src, dst_ref=dst, send_sem=send_sem.at[n], recv_sem=recv_sem.at[n],
            device_id=there, device_id_type=MESH,
        ).start()

    sent = pl.ds(0, TOK_SENT)

    def send_kv(n, s, part):
        for d in (2, 1, 3):
            for c, line, place in ((0, along_x, x), (1, along_y, y)):
                src, dst = kv_own.at[2 * PAIRS[s] + c, part], kv_buf.at[s, 2 * place + core, part, sent]
                send(src, dst, (kv_send, kv_recv), n, line(d, c))
        place = jnp.where(even, y, x)
        src, dst = kv_own.at[2 * PAIRS[s] + 1 - core, part], kv_buf.at[s, 2 * place + core, part, sent]
        send(src, dst, (kv_send, kv_recv), n, other_core)

    def send_q(n, stages):
        for d in (2, 1, 3):
            for c, line, place in ((0, along_y, y), (1, along_x, x)):
                src, dst = q_own.at[c, stages], q_buf.at[2 * place + core, stages]
                send(src, dst, (q_send, q_recv), n, line(d, c))
        place = jnp.where(even, x, y)
        src, dst = q_own.at[1 - core, stages], q_buf.at[2 * place + core, stages]
        send(src, dst, (q_send, q_recv), n, other_core)

    both = slice(None)
    later = pl.ds(1, STAGES - 1)
    send_kv(0, 0, 0)
    send_q(0, 0)
    send_kv(1, 0, 1)
    send_q(1, later)
    send_kv(2, 1, both)

    def tell(n, there):
        pl.semaphore_signal(z_met.at[n], inc=1, device_id=device(x, y, core, there), device_id_type=MESH)

    def pass_on(n, step):
        for d in (-step, step):

            @pl.when(near(d))
            def _():
                tell(n, z + d)

    def told(n, step):
        count = jnp.where(near(-step), 1, 0) + jnp.where(near(step), 1, 0)

        @pl.when(late & (count > 0))
        def _():
            pl.semaphore_wait(z_met.at[n], count)

    pass_on(0, 2)
    for n in range(FIRST_LATE - 1):

        @pl.when((n < z) & (z < FIRST_LATE))
        def _():
            tell(3, n)

    for copy in own[2:]:
        copy.wait()
    lanes = lax.broadcasted_iota(jnp.int32, (GROUP, SEG), 1)
    valid = jnp.where((lanes < TOK) & (z * TOK + lanes < IMG_TOK), 0.0, NEG)
    first_slot = jnp.where(even, 2 * y, 2 * SIDE * x)
    step = jnp.where(even, 2 * SIDE, 2)

    @pl.loop(0, LINE)
    def _(n):
        place = lax.div(n, 2)
        chip = jnp.where(even, x * SIDE + place, place * SIDE + y)
        for r in range(2):
            request = 4 * chip + 2 * lax.rem(n, 2) + r
            cited = count_ref[request]
            named = [jnp.where(j < cited, slot_ref[lists_ref[j, request]], -1) for j in range(LISTS)]
            for m in range(LINE):
                slot = first_slot + step * (m // 2) + m % 2
                hit = jnp.int32(0)
                for name in named:
                    hit = hit + jnp.where(name == slot, 1, 0)
                level = jnp.where(hit > 0, 0.0, NEG)
                bias[n, r * GROUP : (r + 1) * GROUP, m * SEG : (m + 1) * SEG] = valid + level

    told(0, 2)
    pass_on(1, 4)

    others = pl.ds(0, LINE - 1)
    lane = lax.broadcasted_iota(jnp.int32, (LINE, GROUP, HD), 2)

    def work(s):
        if s == 0:
            wait_bytes(q_buf.at[others, 0], q_recv.at[0])
            wait_bytes(kv_buf.at[0, others, 0, sent], kv_recv.at[0])
        else:
            if s == 1:
                wait_bytes(q_buf.at[others, later], q_recv.at[1])
            wait_bytes(kv_buf.at[s, others, :, sent], kv_recv.at[s + 1])
        queries = q_buf[:, s].reshape(LINE * ROWS, HD)
        keys = kv_buf[s, :, 0].reshape(LINE * SEG, HD)
        scores = lax.dot_general(
            queries, keys, (((1,), (1,)), ((), ())), preferred_element_type=jnp.float32
        )
        scores = scores * SCALE + bias[...].reshape(LINE * ROWS, LINE * SEG)
        peak = jnp.max(scores, axis=1, keepdims=True)
        weights = jnp.exp2(scores - peak)
        total = jnp.sum(weights, axis=1, keepdims=True)
        high = weights.astype(jnp.bfloat16)
        low = (weights - high.astype(jnp.float32)).astype(jnp.bfloat16)
        if s == 0:
            wait_bytes(kv_buf.at[0, others, 1, sent], kv_recv.at[1])
        values = kv_buf[s, :, 1].reshape(LINE * SEG, HD)
        weighted = jnp.dot(high, values, preferred_element_type=jnp.float32)
        weighted += jnp.dot(low, values, preferred_element_type=jnp.float32)
        home_out[s, :, :ROWS, :] = (weighted / total).reshape(LINE, ROWS, HD)
        size = (peak + jnp.log2(total)).reshape(LINE, 2, GROUP, 1)
        stat = jnp.where(lane == 0, size[:, 0], jnp.where(lane == 1, size[:, 1], 0.0))
        home_out[s, :, ROWS:, :] = stat
        place = SIDE * core + q_place
        for d in (2, 1, 3):
            there = lax.rem(q_place + d, SIDE)
            for c in range(2):
                to = device(jnp.where(even, x, there), jnp.where(even, there, y), c)
                send(home_out.at[s, 2 * there + c], home_in.at[s, place], (h_send, h_recv), s, to)
        send(home_out.at[s, 2 * q_place + 1 - core], home_in.at[s, place], (h_send, h_recv), s, other_core)
        home_in[s, place] = home_out[s, 2 * q_place + core]

    diagonal = lax.broadcasted_iota(jnp.int32, (GROUP, HD), 0) == lax.broadcasted_iota(jnp.int32, (GROUP, HD), 1)
    low_rows = lax.broadcasted_iota(jnp.int32, (GROUP, HD), 0) < GROUP // 2

    def spread(s):
        wait_bytes(home_in.at[s, others], h_recv.at[s])
        for c in range(2):
            mine = home_in[s, c * SIDE : (c + 1) * SIDE]
            sizes = mine[:, ROWS:, :]
            largest = jnp.max(sizes, axis=0)
            share = jnp.exp2(sizes - largest[None])
            total = jnp.sum(share, axis=0)
            share = share / total[None]
            size = largest + jnp.log2(total)
            results, logs = [], []
            for r in range(2):
                at = r * GROUP
                results.append(jnp.sum(mine[:, at : at + GROUP, :] * share[:, :, r : r + 1], axis=0))
                logs.append(jnp.broadcast_to(size[:, r : r + 1], (GROUP, HD)))
            for h in range(2):
                there = 4 * PAIRS[s] + 2 * c + h
                tiles = []
                for a, b in (results, logs):
                    if h == 0:
                        tiles.append(jnp.where(low_rows, a, pltpu.roll(b, GROUP // 2, 0)))
                    else:
                        tiles.append(jnp.where(low_rows, pltpu.roll(a, GROUP // 2, 0), b))
                z_out[there, :GROUP, :] = tiles[0]
                z_out[there, GROUP:, :] = jnp.sum(jnp.where(diagonal, tiles[1], 0.0), axis=0, keepdims=True)

                @pl.when(z != there)
                def _():
                    pltpu.make_async_remote_copy(
                        src_ref=z_out.at[there], dst_ref=z_in.at[z], send_sem=z_send, recv_sem=z_recv,
                        device_id=device(x, y, core, there), device_id_type=MESH,
                    ).start()

                @pl.when(z == there)
                def _():
                    z_in[z] = z_out[there]

    work(0)

    send_kv(3, 2, both)
    work(1)
    send_kv(4, 3, both)
    told(1, 4)
    for n in range(FIRST_LATE):

        @pl.when(late)
        def _():
            tell(2, n)

    @pl.when(z < FIRST_LATE - 1)
    def _():
        pl.semaphore_wait(z_met.at[3], FIRST_LATE - 1 - z)

    spread(0)
    work(2)
    spread(1)
    work(3)

    @pl.when(z < FIRST_LATE)
    def _():
        pl.semaphore_wait(z_met.at[2], NZ - FIRST_LATE)

    spread(2)
    spread(3)

    wait_bytes(z_in.at[pl.ds(0, NZ - 1)], z_recv)
    sizes = jnp.sum(jnp.where(diagonal[None], z_in[:, GROUP:, :], 0.0), axis=2, keepdims=True)
    largest = jnp.max(sizes, axis=0)
    share = jnp.exp2(sizes - largest[None])
    out_ref[...] = jnp.sum(z_in[:, :GROUP, :] * share, axis=0) / jnp.sum(share, axis=0)

    wait_bytes(q_buf.at[others, 0], q_send.at[0])
    wait_bytes(q_buf.at[others, later], q_send.at[1])
    for i in range(2):
        wait_bytes(kv_buf.at[0, others, i, sent], kv_send.at[i])
    for s in range(1, STAGES):
        wait_bytes(kv_buf.at[s, others, :, sent], kv_send.at[s + 1])
    for s in range(STAGES):
        wait_bytes(home_in.at[s, others], h_send.at[s])
    wait_bytes(z_in.at[pl.ds(0, NZ - 1)], z_send)


def per_device(queries, image_cache, image_lists, cited_count, image_slot):
    home = (STAGES, LINE, ROWS + GROUP, HD)
    along_z = (NZ, GROUP + 1, HD)
    result = pl.pallas_call(
        kernel,
        name="attend",
        out_shape=pltpu.VMEM((GROUP, HD), jnp.float32),
        in_specs=[pl.BlockSpec(memory_space=pl.ANY)] * 5,
        out_specs=pl.BlockSpec(memory_space=pltpu.VMEM),
        scratch_shapes=[
            pltpu.VMEM(queries.shape, jnp.bfloat16),
            pltpu.VMEM(image_cache.shape, jnp.bfloat16),
            pltpu.SMEM((LISTS, REQS), jnp.int32),
            pltpu.SMEM((REQS,), jnp.int32),
            pltpu.SMEM((IMAGES,), jnp.int32),
            pltpu.VMEM((2, STAGES, ROWS, HD), jnp.bfloat16),
            pltpu.VMEM((KVH, 2, TOK_SENT, HD), jnp.bfloat16),
            pltpu.VMEM((LINE, STAGES, ROWS, HD), jnp.bfloat16),
            pltpu.VMEM((STAGES, LINE, 2, SEG, HD), jnp.bfloat16),
            pltpu.VMEM((LINE, ROWS, LINE * SEG), jnp.float32),
            pltpu.VMEM(home, jnp.float32),
            pltpu.VMEM(home, jnp.float32),
            pltpu.VMEM(along_z, jnp.float32),
            pltpu.VMEM(along_z, jnp.float32),
            pltpu.SemaphoreType.DMA((5,)),
            pltpu.SemaphoreType.DMA((2,)),
            pltpu.SemaphoreType.DMA((2,)),
            pltpu.SemaphoreType.DMA((STAGES + 1,)),
            pltpu.SemaphoreType.DMA((STAGES + 1,)),
            pltpu.SemaphoreType.DMA((STAGES,)),
            pltpu.SemaphoreType.DMA((STAGES,)),
            pltpu.SemaphoreType.DMA,
            pltpu.SemaphoreType.DMA,
            pltpu.SemaphoreType.REGULAR((4,)),
        ],
        compiler_params=pltpu.CompilerParams(
            collective_id=0, has_side_effects=True, vmem_limit_bytes=60 * 2**20
        ),
    )(queries, image_cache, image_lists.T, cited_count, image_slot)
    return result.reshape(2, GROUP // 2 * HD)


def solution(mesh):
    return jax.shard_map(
        per_device,
        mesh=mesh,
        in_specs=(P("req", None), P("req", "tp", None), P(), P(), P()),
        out_specs=P("req", "tp"),
        check_vma=False,
    )
```

time: 247 us -> 32.1 us (0.13)
  the two profiles are of different devices: /device:TPU:14 before, /device:TPU:1 now
where the time goes in v4:
time: 32.1 us; the launch traced here: 32 us
  Pallas kernels  31.4 us (98%)
  local copies, waits for them, and re-layouts  0.6 us (2%)
    pallas_call x1, Pallas kernels, per_device(): pl.pallas_call(kernel, name='attend', out_shape=pltpu.VMEM((GROUP, HD), j...  31.4 us

profile of v4, /device:TPU:1, one launch (start us, length us, event | category | flops | bytes accessed | tf_op | source)
XLA Modules:
  0.0 32.0 jit_solution(1932517912979495552)
XLA Ops:
  0.0 31.4 %attend.1 = f32[8,128]{1,0:T(8,128)S(1)} custom-call(bf16[2,8192]{1,0:T(2,128)(2,1)} %q_hbm.1, bf16[1,104,2048]{2,1,0:T(8,128)(2,1)} %cache_hbm.1, s32[4,64]{1,0:T(4,128)} %bitcast.1, s32[64]{0:T(128)} %count_hbm.1, s32[32]{0:T(128)} %slot_hbm.1), custom_call_target="tpu_custom_call" | custom-call | tf_op jit(solution)/shard_map/attend/pallas_call | solution.py:346
  31.4 0.6 %reshape.3 = f32[2,512]{1,0:T(2,128)} reshape(f32[8,128]{1,0:T(8,128)S(1)} %attend.1) | data formatting | bytes 8192 | tf_op jit(solution)/shard_map/reshape | solution.py:382

commit v5 on v4

v5 whole, which is shorter than its diff:
```python
import math

import jax
import jax.numpy as jnp
from jax import lax
from jax.experimental import pallas as pl
from jax.experimental.pallas import tpu as pltpu
from jax.sharding import PartitionSpec as P

KVH = 8
GROUP = 8
HD = 128
IMG_TOK = 1601
LISTS = 4
SIDE = 4
NZ = 16
REQS = 64
IMAGES = 32
TOK = 104
TOK_SENT = 112
SEG = 128
LINE = 2 * SIDE
ROWS = 16
STAGES = (0, 1, 2, 3, 6, 7, 4, 5)
AHEAD = 3
NEG = -1e30
SCALE = math.log2(math.e) / math.sqrt(HD)
MESH = pl.DeviceIdType.MESH
FIRST_LATE = NZ // 2
GREETED = tuple(min(n, 8) if n < 12 else 7 if n == 12 else 6 for n in range(NZ))


def wait_bytes(ref, sem):
    pltpu.make_async_copy(ref, ref, sem).wait()


def kernel(
    q_hbm, cache_hbm, lists_hbm, count_hbm, slot_hbm, out_ref,
    q_ref, cache_ref, lists_ref, count_ref, slot_ref,
    q_own, q_buf, kv_buf, bias, home_out, home_in, z_out, z_in,
    own_sem, q_send, q_recv, kv_send, kv_recv, h_send, h_recv, z_send, z_recv, z_met,
):
    req = lax.axis_index("req")
    z = lax.axis_index("tp")
    core = lax.rem(req, 2)
    x = lax.div(req, 2 * SIDE)
    y = lax.rem(lax.div(req, 2), SIDE)
    even = core == 0

    def device(x_, y_, c_, z_=z):
        return ((x_ * SIDE + y_) * 2 + c_, z_)

    def along_x(d, c_):
        return device(lax.rem(x + d, SIDE), y, c_)

    def along_y(d, c_):
        return device(x, lax.rem(y + d, SIDE), c_)

    def along_z(d):
        return device(x, y, core, lax.rem(z + d + NZ, NZ))

    other_core = device(x, y, 1 - core)
    kv_place = jnp.where(even, x, y)
    q_place = jnp.where(even, y, x)

    barrier = pltpu.get_barrier_semaphore()
    met = [line(d, c_) for d in (2, 1, 3) for line in (along_x, along_y) for c_ in range(2)]
    met += [other_core]
    for there in met:
        pl.semaphore_signal(barrier, inc=1, device_id=there, device_id_type=MESH)
    late = z >= FIRST_LATE

    def near(d):
        return late & (z + d >= FIRST_LATE) & (z + d < NZ)

    for d in (-2, -1, 1, 2):

        @pl.when(near(d))
        def _():
            pl.semaphore_signal(barrier, inc=1, device_id=along_z(d), device_id_type=MESH)

    for n in range(NZ - 1, 0, -1):

        @pl.when(z < GREETED[n])
        def _():
            there = device(x, y, core, n)
            pl.semaphore_signal(barrier, inc=1, device_id=there, device_id_type=MESH)

    own = [
        pltpu.make_async_copy(src, dst, own_sem.at[i])
        for i, (src, dst) in enumerate(
            (
                (q_hbm, q_ref),
                (cache_hbm, cache_ref),
                (lists_hbm, lists_ref),
                (count_hbm, count_ref),
                (slot_hbm, slot_ref),
            )
        )
    ]
    for copy in own:
        copy.start()

    own[0].wait()
    for s, head in enumerate(STAGES):
        first = head * GROUP * HD
        mine = q_ref[:, first : first + GROUP * HD].astype(jnp.float32)
        rows = [mine[r : r + 1, g * HD : (g + 1) * HD] for r in range(2) for g in range(GROUP)]
        q_own[s] = jnp.concatenate(rows, axis=0).astype(jnp.bfloat16)
    q_buf[2 * q_place + core] = q_own[...]

    own[1].wait()
    tail = jnp.zeros((TOK_SENT - TOK, HD), jnp.bfloat16)
    pad = jnp.zeros((SEG - TOK_SENT, HD), jnp.bfloat16)
    for s, head in enumerate(STAGES):
        for i in range(2):
            first = (i * KVH + head) * HD
            block = jnp.concatenate([cache_ref[0, :, first : first + HD], tail], axis=0)
            kv_buf[s, kv_place, i, :TOK_SENT, :] = block
            for n in range(SIDE):
                kv_buf[s, n, i, TOK_SENT:, :] = pad

    greeted = jnp.int32(len(met))
    for d in (-2, -1, 1, 2):
        greeted = greeted + jnp.where(near(d), 1, 0)
    for n in range(1, NZ):
        greeted = greeted + jnp.where(z == n, GREETED[n], 0)
    pl.semaphore_wait(barrier, greeted)

    def send(src, dst, sems, n, there):
        send_sem, recv_sem = sems
        pltpu.make_async_remote_copy(
            src_ref=src, dst_ref=dst, send_sem=send_sem.at[n], recv_sem=recv_sem.at[n],
            device_id=there, device_id_type=MESH,
        ).start()

    sent = pl.ds(0, TOK_SENT)

    def send_kv(n, s, part):
        for d in (2, 1, 3):
            place = lax.rem(kv_place + d, SIDE)
            there = device(jnp.where(even, place, x), jnp.where(even, y, place), core)
            block = kv_buf.at[s, kv_place, part, sent]
            send(block, block, (kv_send, kv_recv), n, there)

    def send_q(n, stages):
        for d in (2, 1, 3):
            for c, line, place in ((0, along_y, y), (1, along_x, x)):
                src, dst = q_own.at[stages], q_buf.at[2 * place + core, stages]
                send(src, dst, (q_send, q_recv), n, line(d, c))
        src, dst = q_own.at[stages], q_buf.at[2 * kv_place + core, stages]
        send(src, dst, (q_send, q_recv), n, other_core)

    both = slice(None)
    soon, later = pl.ds(0, 2), pl.ds(2, KVH - 2)
    send_q(0, soon)
    send_kv(0, 0, 0)
    send_kv(1, 0, 1)
    send_kv(2, 1, both)
    send_q(1, later)
    for s in range(2, AHEAD):
        send_kv(s + 1, s, both)

    def tell(n, there):
        pl.semaphore_signal(z_met.at[n], inc=1, device_id=device(x, y, core, there), device_id_type=MESH)

    def pass_on(n, step):
        for d in (-step, step):

            @pl.when(near(d))
            def _():
                tell(n, z + d)

    def told(n, step):
        count = jnp.where(near(-step), 1, 0) + jnp.where(near(step), 1, 0)

        @pl.when(late & (count > 0))
        def _():
            pl.semaphore_wait(z_met.at[n], count)

    pass_on(0, 2)
    for n in range(FIRST_LATE - 1):

        @pl.when((n < z) & (z < FIRST_LATE))
        def _():
            tell(3, n)

    for copy in own[2:]:
        copy.wait()
    lanes = lax.broadcasted_iota(jnp.int32, (GROUP, SEG), 1)
    valid = jnp.where((lanes < TOK) & (z * TOK + lanes < IMG_TOK), 0.0, NEG)
    first_slot = jnp.where(even, 2 * y, 2 * SIDE * x + 1)
    step = jnp.where(even, 2 * SIDE, 2)

    @pl.loop(0, LINE)
    def _(n):
        place = lax.div(n, 2)
        chip = jnp.where(even, x * SIDE + place, place * SIDE + y)
        for r in range(2):
            request = 4 * chip + 2 * lax.rem(n, 2) + r
            cited = count_ref[request]
            named = [jnp.where(j < cited, slot_ref[lists_ref[j, request]], -1) for j in range(LISTS)]
            for m in range(SIDE):
                slot = first_slot + step * m
                hit = jnp.int32(0)
                for name in named:
                    hit = hit + jnp.where(name == slot, 1, 0)
                level = jnp.where(hit > 0, 0.0, NEG)
                bias[n, r * GROUP : (r + 1) * GROUP, m * SEG : (m + 1) * SEG] = valid + level

    told(0, 2)
    pass_on(1, 4)

    others, line_others = pl.ds(0, LINE - 1), pl.ds(0, SIDE - 1)
    iota = [lax.broadcasted_iota(jnp.int32, (1, 2, GROUP, HD), i) for i in range(4)]
    in_row = iota[3] == iota[1] * GROUP + iota[2]

    def work(s):
        if s == 0:
            wait_bytes(q_buf.at[others, soon], q_recv.at[0])
            wait_bytes(kv_buf.at[0, line_others, 0, sent], kv_recv.at[0])
        else:
            if s == 2:
                wait_bytes(q_buf.at[others, later], q_recv.at[1])
            wait_bytes(kv_buf.at[s, line_others, :, sent], kv_recv.at[s + 1])
        queries = q_buf[:, s].reshape(LINE * ROWS, HD)
        keys = kv_buf[s, :, 0].reshape(SIDE * SEG, HD)
        scores = lax.dot_general(
            queries, keys, (((1,), (1,)), ((), ())), preferred_element_type=jnp.float32
        )
        scores = scores * SCALE + bias[...].reshape(LINE * ROWS, SIDE * SEG)
        peak = jnp.max(scores, axis=1, keepdims=True)
        weights = jnp.exp2(scores - peak)
        total = jnp.sum(weights, axis=1, keepdims=True)
        high = weights.astype(jnp.bfloat16)
        low = (weights - high.astype(jnp.float32)).astype(jnp.bfloat16)
        if s == 0:
            wait_bytes(kv_buf.at[0, line_others, 1, sent], kv_recv.at[1])
        values = kv_buf[s, :, 1].reshape(SIDE * SEG, HD)
        weighted = jnp.dot(high, values, preferred_element_type=jnp.float32)
        weighted += jnp.dot(low, values, preferred_element_type=jnp.float32)
        home_out[s, :, :ROWS, :] = (weighted / total).reshape(LINE, ROWS, HD)
        size = (peak + jnp.log2(total)).reshape(LINE, 2, GROUP, 1)
        row = jnp.sum(jnp.where(in_row, size, 0.0), axis=2, keepdims=True)
        home_out[s, :, ROWS:, :] = jnp.sum(row, axis=1)
        place = SIDE * core + q_place
        for d in (2, 1, 3):
            there = lax.rem(q_place + d, SIDE)
            for c in range(2):
                to = device(jnp.where(even, x, there), jnp.where(even, there, y), c)
                send(home_out.at[s, 2 * there + c], home_in.at[s, place], (h_send, h_recv), s, to)
        send(home_out.at[s, 2 * q_place + 1 - core], home_in.at[s, place], (h_send, h_recv), s, other_core)
        home_in[s, place] = home_out[s, 2 * q_place + core]
        if s + AHEAD < KVH:
            send_kv(s + AHEAD + 1, s + AHEAD, both)

    diagonal = lax.broadcasted_iota(jnp.int32, (GROUP, HD), 0) == lax.broadcasted_iota(jnp.int32, (GROUP, HD), 1)
    low_rows = lax.broadcasted_iota(jnp.int32, (GROUP, HD), 0) < GROUP // 2

    def spread(s):
        wait_bytes(home_in.at[s, others], h_recv.at[s])
        row = home_in[s, :, ROWS:, :].reshape(LINE, 1, 1, HD)
        sizes = jnp.sum(jnp.where(in_row, row, 0.0), axis=3, keepdims=True)
        largest = jnp.max(sizes, axis=0)
        share = jnp.exp2(sizes - largest[None])
        total = jnp.sum(share, axis=0)
        share = share / total[None]
        size = largest + jnp.log2(total)
        results, logs = [], []
        for r in range(2):
            part = home_in[s, :, r * GROUP : (r + 1) * GROUP, :]
            results.append(jnp.sum(part * share[:, r], axis=0))
            logs.append(jnp.broadcast_to(size[r], (GROUP, HD)))
        for h in range(2):
            there = 2 * STAGES[s] + h
            tiles = []
            for a, b in (results, logs):
                if h == 0:
                    tiles.append(jnp.where(low_rows, a, pltpu.roll(b, GROUP // 2, 0)))
                else:
                    tiles.append(jnp.where(low_rows, pltpu.roll(a, GROUP // 2, 0), b))
            z_out[there, :GROUP, :] = tiles[0]
            z_out[there, GROUP:, :] = jnp.sum(jnp.where(diagonal, tiles[1], 0.0), axis=0, keepdims=True)

            @pl.when(z != there)
            def _():
                pltpu.make_async_remote_copy(
                    src_ref=z_out.at[there], dst_ref=z_in.at[z], send_sem=z_send, recv_sem=z_recv,
                    device_id=device(x, y, core, there), device_id_type=MESH,
                ).start()

            @pl.when(z == there)
            def _():
                z_in[z] = z_out[there]

    work(0)
    told(1, 4)
    for n in range(FIRST_LATE):

        @pl.when(late)
        def _():
            tell(2, n)

    for s in range(1, 3):
        work(s)

    @pl.when(z < FIRST_LATE - 1)
    def _():
        pl.semaphore_wait(z_met.at[3], FIRST_LATE - 1 - z)

    spread(0)
    for s in range(1, KVH):
        if s + 3 - 1 < KVH:
            work(s + 3 - 1)
        if STAGES[s] * 2 >= FIRST_LATE and STAGES[s - 1] * 2 < FIRST_LATE:

            @pl.when(z < FIRST_LATE)
            def _():
                pl.semaphore_wait(z_met.at[2], NZ - FIRST_LATE)

        spread(s)

    wait_bytes(z_in.at[pl.ds(0, NZ - 1)], z_recv)
    sizes = jnp.sum(jnp.where(diagonal[None], z_in[:, GROUP:, :], 0.0), axis=2, keepdims=True)
    largest = jnp.max(sizes, axis=0)
    share = jnp.exp2(sizes - largest[None])
    result = jnp.sum(z_in[:, :GROUP, :] * share, axis=0) / jnp.sum(share, axis=0)
    for r in range(2):
        for g in range(GROUP // 2):
            at = r * (GROUP // 2) + g
            out_ref[r : r + 1, g * HD : (g + 1) * HD] = result[at : at + 1]

    wait_bytes(q_buf.at[others, soon], q_send.at[0])
    wait_bytes(q_buf.at[others, later], q_send.at[1])
    for i in range(2):
        wait_bytes(kv_buf.at[0, line_others, i, sent], kv_send.at[i])
    for s in range(1, KVH):
        wait_bytes(kv_buf.at[s, line_others, :, sent], kv_send.at[s + 1])
    for s in range(KVH):
        wait_bytes(home_in.at[s, others], h_send.at[s])
    wait_bytes(z_in.at[pl.ds(0, NZ - 1)], z_send)


def per_device(queries, image_cache, image_lists, cited_count, image_slot):
    home = (KVH, LINE, ROWS + 1, HD)
    along_z = (NZ, GROUP + 1, HD)
    return pl.pallas_call(
        kernel,
        name="attend",
        out_shape=pltpu.VMEM((2, GROUP // 2 * HD), jnp.float32),
        in_specs=[pl.BlockSpec(memory_space=pl.ANY)] * 5,
        out_specs=pl.BlockSpec(memory_space=pltpu.VMEM),
        scratch_shapes=[
            pltpu.VMEM(queries.shape, jnp.bfloat16),
            pltpu.VMEM(image_cache.shape, jnp.bfloat16),
            pltpu.SMEM((LISTS, REQS), jnp.int32),
            pltpu.SMEM((REQS,), jnp.int32),
            pltpu.SMEM((IMAGES,), jnp.int32),
            pltpu.VMEM((KVH, ROWS, HD), jnp.bfloat16),
            pltpu.VMEM((LINE, KVH, ROWS, HD), jnp.bfloat16),
            pltpu.VMEM((KVH, SIDE, 2, SEG, HD), jnp.bfloat16),
            pltpu.VMEM((LINE, ROWS, SIDE * SEG), jnp.float32),
            pltpu.VMEM(home, jnp.float32),
            pltpu.VMEM(home, jnp.float32),
            pltpu.VMEM(along_z, jnp.float32),
            pltpu.VMEM(along_z, jnp.float32),
            pltpu.SemaphoreType.DMA((5,)),
            pltpu.SemaphoreType.DMA((2,)),
            pltpu.SemaphoreType.DMA((2,)),
            pltpu.SemaphoreType.DMA((KVH + 1,)),
            pltpu.SemaphoreType.DMA((KVH + 1,)),
            pltpu.SemaphoreType.DMA((KVH,)),
            pltpu.SemaphoreType.DMA((KVH,)),
            pltpu.SemaphoreType.DMA,
            pltpu.SemaphoreType.DMA,
            pltpu.SemaphoreType.REGULAR((4,)),
        ],
        compiler_params=pltpu.CompilerParams(
            collective_id=0, has_side_effects=True, vmem_limit_bytes=60 * 2**20
        ),
    )(queries, image_cache, image_lists.T, cited_count, image_slot)


def solution(mesh):
    return jax.shard_map(
        per_device,
        mesh=mesh,
        in_specs=(P("req", None), P("req", "tp", None), P(), P(), P()),
        out_specs=P("req", "tp"),
        check_vma=False,
    )
```

time: 32.1 us -> 31.4 us (0.978)
  Pallas kernels: 31.4 us -> 30.7 us
    pallas_call x1, Pallas kernels: 31.4 us -> 30.7 us  [per_device(): pl.pallas_call(kernel, name='attend', out_shape=pltpu.VMEM((2, GROUP // 2...]
    reshape x1 -> x0, local copies, waits for them, and re-layouts: 0.6 us -> none  [per_device(): return result.reshape(2, GROUP // 2 * HD)]
    unnamed x0 -> x1, local copies, waits for them, and re-layouts: none -> 0.6 us
where the time goes in v5:
time: 31.4 us; the launch traced here: 31.3 us
  Pallas kernels  30.7 us (98%)
  local copies, waits for them, and re-layouts  0.6 us (2%)
    pallas_call x1, Pallas kernels, per_device(): pl.pallas_call(kernel, name='attend', out_shape=pltpu.VMEM((2, GROUP // 2...  30.7 us

profile of v5, /device:TPU:1, one launch (start us, length us, event | category | flops | bytes accessed | tf_op | source)
XLA Modules:
  0.0 31.3 jit_solution(10342206388084512258)
XLA Ops:
  0.0 30.7 %attend.1 = f32[2,512]{1,0:T(2,128)S(1)} custom-call(bf16[2,8192]{1,0:T(2,128)(2,1)} %q_hbm.1, bf16[1,104,2048]{2,1,0:T(8,128)(2,1)} %cache_hbm.1, s32[4,64]{1,0:T(4,128)} %bitcast.1, s32[64]{0:T(128)} %count_hbm.1, s32[32]{0:T(128)} %slot_hbm.1), custom_call_target="tpu_custom_call" | custom-call | tf_op jit(solution)/shard_map/attend/pallas_call | solution.py:347
  30.7 0.6 %copy.7 = f32[2,512]{1,0:T(2,128)} copy(f32[2,512]{1,0:T(2,128)S(1)} %attend.1) | data formatting | bytes 8192

commit v6 on v5

--- a/solution.py
+++ b/solution.py
@@ -17,12 +17,9 @@
 REQS = 64
 IMAGES = 32
 TOK = 104
-TOK_SENT = 112
-SEG = 128
 LINE = 2 * SIDE
 ROWS = 16
 STAGES = (0, 1, 2, 3, 6, 7, 4, 5)
-AHEAD = 3
 NEG = -1e30
 SCALE = math.log2(math.e) / math.sqrt(HD)
 MESH = pl.DeviceIdType.MESH
@@ -110,15 +107,10 @@
     q_buf[2 * q_place + core] = q_own[...]
 
     own[1].wait()
-    tail = jnp.zeros((TOK_SENT - TOK, HD), jnp.bfloat16)
-    pad = jnp.zeros((SEG - TOK_SENT, HD), jnp.bfloat16)
     for s, head in enumerate(STAGES):
         for i in range(2):
             first = (i * KVH + head) * HD
-            block = jnp.concatenate([cache_ref[0, :, first : first + HD], tail], axis=0)
-            kv_buf[s, kv_place, i, :TOK_SENT, :] = block
-            for n in range(SIDE):
-                kv_buf[s, n, i, TOK_SENT:, :] = pad
+            kv_buf[s, kv_place, i] = cache_ref[0, :, first : first + HD]
 
     greeted = jnp.int32(len(met))
     for d in (-2, -1, 1, 2):
@@ -134,13 +126,12 @@
             device_id=there, device_id_type=MESH,
         ).start()
 
-    sent = pl.ds(0, TOK_SENT)
 
     def send_kv(n, s, part):
         for d in (2, 1, 3):
             place = lax.rem(kv_place + d, SIDE)
             there = device(jnp.where(even, place, x), jnp.where(even, y, place), core)
-            block = kv_buf.at[s, kv_place, part, sent]
+            block = kv_buf.at[s, kv_place, part]
             send(block, block, (kv_send, kv_recv), n, there)
 
     def send_q(n, stages):
@@ -158,8 +149,8 @@
     send_kv(1, 0, 1)
     send_kv(2, 1, both)
     send_q(1, later)
-    for s in range(2, AHEAD):
-        send_kv(s + 1, s, both)
+    send_kv(3, 2, both)
+    send_kv(4, 3, both)
 
     def tell(n, there):
         pl.semaphore_signal(z_met.at[n], inc=1, device_id=device(x, y, core, there), device_id_type=MESH)
@@ -187,8 +178,9 @@
 
     for copy in own[2:]:
         copy.wait()
-    lanes = lax.broadcasted_iota(jnp.int32, (GROUP, SEG), 1)
-    valid = jnp.where((lanes < TOK) & (z * TOK + lanes < IMG_TOK), 0.0, NEG)
+    lanes = lax.broadcasted_iota(jnp.int32, (GROUP, SIDE * TOK), 1)
+    image = sum(jnp.where(lanes >= m * TOK, 1, 0) for m in range(1, SIDE))
+    valid = jnp.where(z * TOK + lanes - image * TOK < IMG_TOK, 0.0, NEG)
     first_slot = jnp.where(even, 2 * y, 2 * SIDE * x + 1)
     step = jnp.where(even, 2 * SIDE, 2)
 
@@ -200,13 +192,14 @@
             request = 4 * chip + 2 * lax.rem(n, 2) + r
             cited = count_ref[request]
             named = [jnp.where(j < cited, slot_ref[lists_ref[j, request]], -1) for j in range(LISTS)]
+            level = valid
             for m in range(SIDE):
                 slot = first_slot + step * m
                 hit = jnp.int32(0)
                 for name in named:
                     hit = hit + jnp.where(name == slot, 1, 0)
-                level = jnp.where(hit > 0, 0.0, NEG)
-                bias[n, r * GROUP : (r + 1) * GROUP, m * SEG : (m + 1) * SEG] = valid + level
+                level = level + jnp.where(image == m, jnp.where(hit > 0, 0.0, NEG), 0.0)
+            bias[n, r * GROUP : (r + 1) * GROUP, :] = level
 
     told(0, 2)
     pass_on(1, 4)
@@ -218,25 +211,25 @@
     def work(s):
         if s == 0:
             wait_bytes(q_buf.at[others, soon], q_recv.at[0])
-            wait_bytes(kv_buf.at[0, line_others, 0, sent], kv_recv.at[0])
+            wait_bytes(kv_buf.at[0, line_others, 0], kv_recv.at[0])
         else:
             if s == 2:
                 wait_bytes(q_buf.at[others, later], q_recv.at[1])
-            wait_bytes(kv_buf.at[s, line_others, :, sent], kv_recv.at[s + 1])
+            wait_bytes(kv_buf.at[s, line_others], kv_recv.at[s + 1])
         queries = q_buf[:, s].reshape(LINE * ROWS, HD)
-        keys = kv_buf[s, :, 0].reshape(SIDE * SEG, HD)
+        keys = kv_buf[s, :, 0].reshape(SIDE * TOK, HD)
         scores = lax.dot_general(
             queries, keys, (((1,), (1,)), ((), ())), preferred_element_type=jnp.float32
         )
-        scores = scores * SCALE + bias[...].reshape(LINE * ROWS, SIDE * SEG)
+        scores = scores * SCALE + bias[...].reshape(LINE * ROWS, SIDE * TOK)
         peak = jnp.max(scores, axis=1, keepdims=True)
         weights = jnp.exp2(scores - peak)
         total = jnp.sum(weights, axis=1, keepdims=True)
         high = weights.astype(jnp.bfloat16)
         low = (weights - high.astype(jnp.float32)).astype(jnp.bfloat16)
         if s == 0:
-            wait_bytes(kv_buf.at[0, line_others, 1, sent], kv_recv.at[1])
-        values = kv_buf[s, :, 1].reshape(SIDE * SEG, HD)
+            wait_bytes(kv_buf.at[0, line_others, 1], kv_recv.at[1])
+        values = kv_buf[s, :, 1].reshape(SIDE * TOK, HD)
         weighted = jnp.dot(high, values, preferred_element_type=jnp.float32)
         weighted += jnp.dot(low, values, preferred_element_type=jnp.float32)
         home_out[s, :, :ROWS, :] = (weighted / total).reshape(LINE, ROWS, HD)
@@ -251,8 +244,6 @@
                 send(home_out.at[s, 2 * there + c], home_in.at[s, place], (h_send, h_recv), s, to)
         send(home_out.at[s, 2 * q_place + 1 - core], home_in.at[s, place], (h_send, h_recv), s, other_core)
         home_in[s, place] = home_out[s, 2 * q_place + core]
-        if s + AHEAD < KVH:
-            send_kv(s + AHEAD + 1, s + AHEAD, both)
 
     diagonal = lax.broadcasted_iota(jnp.int32, (GROUP, HD), 0) == lax.broadcasted_iota(jnp.int32, (GROUP, HD), 1)
     low_rows = lax.broadcasted_iota(jnp.int32, (GROUP, HD), 0) < GROUP // 2
@@ -294,6 +285,7 @@
                 z_in[z] = z_out[there]
 
     work(0)
+    send_kv(5, 4, both)
     told(1, 4)
     for n in range(FIRST_LATE):
 
@@ -301,24 +293,32 @@
         def _():
             tell(2, n)
 
-    for s in range(1, 3):
-        work(s)
-
+    work(1)
+    send_kv(6, 5, both)
+    work(2)
+    send_kv(7, 6, both)
     @pl.when(z < FIRST_LATE - 1)
     def _():
         pl.semaphore_wait(z_met.at[3], FIRST_LATE - 1 - z)
 
     spread(0)
-    for s in range(1, KVH):
-        if s + 3 - 1 < KVH:
-            work(s + 3 - 1)
-        if STAGES[s] * 2 >= FIRST_LATE and STAGES[s - 1] * 2 < FIRST_LATE:
-
-            @pl.when(z < FIRST_LATE)
-            def _():
-                pl.semaphore_wait(z_met.at[2], NZ - FIRST_LATE)
-
-        spread(s)
+    work(3)
+    send_kv(8, 7, both)
+    spread(1)
+    work(4)
+    spread(2)
+    work(5)
+    spread(3)
+    work(6)
+    work(7)
+    @pl.when(z < FIRST_LATE)
+    def _():
+        pl.semaphore_wait(z_met.at[2], NZ - FIRST_LATE)
+
+    spread(4)
+    spread(5)
+    spread(6)
+    spread(7)
 
     wait_bytes(z_in.at[pl.ds(0, NZ - 1)], z_recv)
     sizes = jnp.sum(jnp.where(diagonal[None], z_in[:, GROUP:, :], 0.0), axis=2, keepdims=True)
@@ -333,9 +333,9 @@
     wait_bytes(q_buf.at[others, soon], q_send.at[0])
     wait_bytes(q_buf.at[others, later], q_send.at[1])
     for i in range(2):
-        wait_bytes(kv_buf.at[0, line_others, i, sent], kv_send.at[i])
+        wait_bytes(kv_buf.at[0, line_others, i], kv_send.at[i])
     for s in range(1, KVH):
-        wait_bytes(kv_buf.at[s, line_others, :, sent], kv_send.at[s + 1])
+        wait_bytes(kv_buf.at[s, line_others], kv_send.at[s + 1])
     for s in range(KVH):
         wait_bytes(home_in.at[s, others], h_send.at[s])
     wait_bytes(z_in.at[pl.ds(0, NZ - 1)], z_send)
@@ -358,8 +358,8 @@
             pltpu.SMEM((IMAGES,), jnp.int32),
             pltpu.VMEM((KVH, ROWS, HD), jnp.bfloat16),
             pltpu.VMEM((LINE, KVH, ROWS, HD), jnp.bfloat16),
-            pltpu.VMEM((KVH, SIDE, 2, SEG, HD), jnp.bfloat16),
-            pltpu.VMEM((LINE, ROWS, SIDE * SEG), jnp.float32),
+            pltpu.VMEM((KVH, SIDE, 2, TOK, HD), jnp.bfloat16),
+            pltpu.VMEM((LINE, ROWS, SIDE * TOK), jnp.float32),
             pltpu.VMEM(home, jnp.float32),
             pltpu.VMEM(home, jnp.float32),
             pltpu.VMEM(along_z, jnp.float32),

time: 31.4 us -> 31 us (0.987)
  Pallas kernels: 30.7 us -> 30.3 us
    pallas_call x1, Pallas kernels: 30.7 us -> 30.3 us  [per_device(): pl.pallas_call(kernel, name='attend', out_shape=pltpu.VMEM((2, GROUP // 2...]
where the time goes in v6:
time: 31 us; the launch traced here: 30.9 us
  Pallas kernels  30.3 us (98%)
  local copies, waits for them, and re-layouts  0.6 us (2%)
    pallas_call x1, Pallas kernels, per_device(): pl.pallas_call(kernel, name='attend', out_shape=pltpu.VMEM((2, GROUP // 2...  30.3 us

profile of v6, /device:TPU:1, one launch (start us, length us, event | category | flops | bytes accessed | tf_op | source)
XLA Modules:
  0.0 30.9 jit_solution(10183461499843985437)
XLA Ops:
  0.0 30.3 %attend.1 = f32[2,512]{1,0:T(2,128)S(1)} custom-call(bf16[2,8192]{1,0:T(2,128)(2,1)} %q_hbm.1, bf16[1,104,2048]{2,1,0:T(8,128)(2,1)} %cache_hbm.1, s32[4,64]{1,0:T(4,128)} %bitcast.1, s32[64]{0:T(128)} %count_hbm.1, s32[32]{0:T(128)} %slot_hbm.1), custom_call_target="tpu_custom_call" | custom-call | tf_op jit(solution)/shard_map/attend/pallas_call | solution.py:347
  30.3 0.6 %copy.7 = f32[2,512]{1,0:T(2,128)} copy(f32[2,512]{1,0:T(2,128)S(1)} %attend.1) | data formatting | bytes 8192

commit v7 on v6

--- a/solution.py
+++ b/solution.py
@@ -65,24 +65,6 @@
     met += [other_core]
     for there in met:
         pl.semaphore_signal(barrier, inc=1, device_id=there, device_id_type=MESH)
-    late = z >= FIRST_LATE
-
-    def near(d):
-        return late & (z + d >= FIRST_LATE) & (z + d < NZ)
-
-    for d in (-2, -1, 1, 2):
-
-        @pl.when(near(d))
-        def _():
-            pl.semaphore_signal(barrier, inc=1, device_id=along_z(d), device_id_type=MESH)
-
-    for n in range(NZ - 1, 0, -1):
-
-        @pl.when(z < GREETED[n])
-        def _():
-            there = device(x, y, core, n)
-            pl.semaphore_signal(barrier, inc=1, device_id=there, device_id_type=MESH)
-
     own = [
         pltpu.make_async_copy(src, dst, own_sem.at[i])
         for i, (src, dst) in enumerate(
@@ -97,6 +79,24 @@
     ]
     for copy in own:
         copy.start()
+
+    late = z >= FIRST_LATE
+
+    def near(d):
+        return late & (z + d >= FIRST_LATE) & (z + d < NZ)
+
+    for d in (-2, -1, 1, 2):
+
+        @pl.when(near(d))
+        def _():
+            pl.semaphore_signal(barrier, inc=1, device_id=along_z(d), device_id_type=MESH)
+
+    for n in range(NZ - 1, 0, -1):
+
+        @pl.when(z < GREETED[n])
+        def _():
+            there = device(x, y, core, n)
+            pl.semaphore_signal(barrier, inc=1, device_id=there, device_id_type=MESH)
 
     own[0].wait()
     for s, head in enumerate(STAGES):
@@ -286,6 +286,8 @@
 
     work(0)
     send_kv(5, 4, both)
+    work(1)
+    send_kv(6, 5, both)
     told(1, 4)
     for n in range(FIRST_LATE):
 
@@ -293,8 +295,6 @@
         def _():
             tell(2, n)
 
-    work(1)
-    send_kv(6, 5, both)
     work(2)
     send_kv(7, 6, both)
     @pl.when(z < FIRST_LATE - 1)
@@ -320,6 +320,15 @@
     spread(6)
     spread(7)
 
+    wait_bytes(q_buf.at[others, soon], q_send.at[0])
+    wait_bytes(q_buf.at[others, later], q_send.at[1])
+    for i in range(2):
+        wait_bytes(kv_buf.at[0, line_others, i], kv_send.at[i])
+    for s in range(1, KVH):
+        wait_bytes(kv_buf.at[s, line_others], kv_send.at[s + 1])
+    for s in range(KVH):
+        wait_bytes(home_in.at[s, others], h_send.at[s])
+
     wait_bytes(z_in.at[pl.ds(0, NZ - 1)], z_recv)
     sizes = jnp.sum(jnp.where(diagonal[None], z_in[:, GROUP:, :], 0.0), axis=2, keepdims=True)
     largest = jnp.max(sizes, axis=0)
@@ -330,14 +339,6 @@
             at = r * (GROUP // 2) + g
             out_ref[r : r + 1, g * HD : (g + 1) * HD] = result[at : at + 1]
 
-    wait_bytes(q_buf.at[others, soon], q_send.at[0])
-    wait_bytes(q_buf.at[others, later], q_send.at[1])
-    for i in range(2):
-        wait_bytes(kv_buf.at[0, line_others, i], kv_send.at[i])
-    for s in range(1, KVH):
-        wait_bytes(kv_buf.at[s, line_others], kv_send.at[s + 1])
-    for s in range(KVH):
-        wait_bytes(home_in.at[s, others], h_send.at[s])
     wait_bytes(z_in.at[pl.ds(0, NZ - 1)], z_send)
 
 

time: 31 us -> 31 us (level)
  no operation moved by 1% of the time
where the time goes in v7:
time: 31 us; the launch traced here: 30.8 us
  Pallas kernels  30.2 us (97%)
  local copies, waits for them, and re-layouts  0.6 us (2%)
    pallas_call x1, Pallas kernels, per_device(): pl.pallas_call(kernel, name='attend', out_shape=pltpu.VMEM((2, GROUP // 2...  30.2 us

profile of v7, /device:TPU:1, one launch (start us, length us, event | category | flops | bytes accessed | tf_op | source)
XLA Modules:
  0.0 30.8 jit_solution(12351603036441142841)
XLA Ops:
  0.0 30.2 %attend.1 = f32[2,512]{1,0:T(2,128)S(1)} custom-call(bf16[2,8192]{1,0:T(2,128)(2,1)} %q_hbm.1, bf16[1,104,2048]{2,1,0:T(8,128)(2,1)} %cache_hbm.1, s32[4,64]{1,0:T(4,128)} %bitcast.1, s32[64]{0:T(128)} %count_hbm.1, s32[32]{0:T(128)} %slot_hbm.1), custom_call_target="tpu_custom_call" | custom-call | tf_op jit(solution)/shard_map/attend/pallas_call | solution.py:348
  30.3 0.6 %copy.7 = f32[2,512]{1,0:T(2,128)} copy(f32[2,512]{1,0:T(2,128)S(1)} %attend.1) | data formatting | bytes 8192

commit v8 on v7

--- a/solution.py
+++ b/solution.py
@@ -143,7 +143,7 @@
         send(src, dst, (q_send, q_recv), n, other_core)
 
     both = slice(None)
-    soon, later = pl.ds(0, 2), pl.ds(2, KVH - 2)
+    soon, later = pl.ds(0, 1), pl.ds(1, KVH - 1)
     send_q(0, soon)
     send_kv(0, 0, 0)
     send_kv(1, 0, 1)
@@ -213,7 +213,7 @@
             wait_bytes(q_buf.at[others, soon], q_recv.at[0])
             wait_bytes(kv_buf.at[0, line_others, 0], kv_recv.at[0])
         else:
-            if s == 2:
+            if s == 1:
                 wait_bytes(q_buf.at[others, later], q_recv.at[1])
             wait_bytes(kv_buf.at[s, line_others], kv_recv.at[s + 1])
         queries = q_buf[:, s].reshape(LINE * ROWS, HD)

time: 31 us -> 30.9 us (level)
  no operation moved by 1% of the time
where the time goes in v8:
time: 30.9 us; the launch traced here: 30.8 us
  Pallas kernels  30.2 us (98%)
  local copies, waits for them, and re-layouts  0.6 us (2%)
    pallas_call x1, Pallas kernels, per_device(): pl.pallas_call(kernel, name='attend', out_shape=pltpu.VMEM((2, GROUP // 2...  30.2 us

profile of v8, /device:TPU:1, one launch (start us, length us, event | category | flops | bytes accessed | tf_op | source)
XLA Modules:
  0.0 30.8 jit_solution(347185486228957367)
XLA Ops:
  0.0 30.2 %attend.1 = f32[2,512]{1,0:T(2,128)S(1)} custom-call(bf16[2,8192]{1,0:T(2,128)(2,1)} %q_hbm.1, bf16[1,104,2048]{2,1,0:T(8,128)(2,1)} %cache_hbm.1, s32[4,64]{1,0:T(4,128)} %bitcast.1, s32[64]{0:T(128)} %count_hbm.1, s32[32]{0:T(128)} %slot_hbm.1), custom_call_target="tpu_custom_call" | custom-call | tf_op jit(solution)/shard_map/attend/pallas_call | solution.py:348
  30.2 0.6 %copy.7 = f32[2,512]{1,0:T(2,128)} copy(f32[2,512]{1,0:T(2,128)S(1)} %attend.1) | data formatting | bytes 8192

commit v9 on v8

--- a/solution.py
+++ b/solution.py
@@ -143,12 +143,13 @@
         send(src, dst, (q_send, q_recv), n, other_core)
 
     both = slice(None)
-    soon, later = pl.ds(0, 1), pl.ds(1, KVH - 1)
+    soon, second, later = pl.ds(0, 1), pl.ds(1, 1), pl.ds(2, KVH - 2)
     send_q(0, soon)
     send_kv(0, 0, 0)
     send_kv(1, 0, 1)
+    send_q(1, second)
     send_kv(2, 1, both)
-    send_q(1, later)
+    send_q(2, later)
     send_kv(3, 2, both)
     send_kv(4, 3, both)
 
@@ -214,7 +215,9 @@
             wait_bytes(kv_buf.at[0, line_others, 0], kv_recv.at[0])
         else:
             if s == 1:
-                wait_bytes(q_buf.at[others, later], q_recv.at[1])
+                wait_bytes(q_buf.at[others, second], q_recv.at[1])
+            if s == 2:
+                wait_bytes(q_buf.at[others, later], q_recv.at[2])
             wait_bytes(kv_buf.at[s, line_others], kv_recv.at[s + 1])
         queries = q_buf[:, s].reshape(LINE * ROWS, HD)
         keys = kv_buf[s, :, 0].reshape(SIDE * TOK, HD)
@@ -321,7 +324,8 @@
     spread(7)
 
     wait_bytes(q_buf.at[others, soon], q_send.at[0])
-    wait_bytes(q_buf.at[others, later], q_send.at[1])
+    wait_bytes(q_buf.at[others, second], q_send.at[1])
+    wait_bytes(q_buf.at[others, later], q_send.at[2])
     for i in range(2):
         wait_bytes(kv_buf.at[0, line_others, i], kv_send.at[i])
     for s in range(1, KVH):
@@ -366,8 +370,8 @@
             pltpu.VMEM(along_z, jnp.float32),
             pltpu.VMEM(along_z, jnp.float32),
             pltpu.SemaphoreType.DMA((5,)),
-            pltpu.SemaphoreType.DMA((2,)),
-            pltpu.SemaphoreType.DMA((2,)),
+            pltpu.SemaphoreType.DMA((3,)),
+            pltpu.SemaphoreType.DMA((3,)),
             pltpu.SemaphoreType.DMA((KVH + 1,)),
             pltpu.SemaphoreType.DMA((KVH + 1,)),
             pltpu.SemaphoreType.DMA((KVH,)),

time: 30.9 us -> 30.9 us (level)
  no operation moved by 1% of the time
where the time goes in v9:
time: 30.9 us; the launch traced here: 30.8 us
  Pallas kernels  30.2 us (98%)
  local copies, waits for them, and re-layouts  0.6 us (2%)
    pallas_call x1, Pallas kernels, per_device(): pl.pallas_call(kernel, name='attend', out_shape=pltpu.VMEM((2, GROUP // 2...  30.2 us

profile of v9, /device:TPU:1, one launch (start us, length us, event | category | flops | bytes accessed | tf_op | source)
XLA Modules:
  0.0 30.8 jit_solution(7945288268040087568)
XLA Ops:
  0.0 30.2 %attend.1 = f32[2,512]{1,0:T(2,128)S(1)} custom-call(bf16[2,8192]{1,0:T(2,128)(2,1)} %q_hbm.1, bf16[1,104,2048]{2,1,0:T(8,128)(2,1)} %cache_hbm.1, s32[4,64]{1,0:T(4,128)} %bitcast.1, s32[64]{0:T(128)} %count_hbm.1, s32[32]{0:T(128)} %slot_hbm.1), custom_call_target="tpu_custom_call" | custom-call | tf_op jit(solution)/shard_map/attend/pallas_call | solution.py:352
  30.2 0.6 %copy.7 = f32[2,512]{1,0:T(2,128)} copy(f32[2,512]{1,0:T(2,128)S(1)} %attend.1) | data formatting | bytes 8192
